TPU v7x, 512 devices: a whole 4x4x16 slice. The times are simulated.
512 devices in a mesh: outer: 32 (over z, core), inner: 16 (over y, x).
Axes of the slice: x: 4, y: 4, z: 16, core: 2. Of those that a mesh axis runs over, the one named last changes fastest.
Arguments:
- tokens: bfloat16 [4096, 4096], P('outer', 'inner'), may hold values from -6 to 6
- routes: int32 [4096, 8], P('outer'), may hold values from 0 to 127, all different within a row; in each aligned block of 128 rows (0 to 127, 128 to 255, ...) at most 10 rows name the same one
- gates: float32 [4096, 8], P('outer'), may hold values from 0.1 to 1
- w_gate_up: bfloat16 [128, 4096, 1536], P('outer', 'inner'), may hold values from -0.09375 to 0.09375
- w_down: bfloat16 [128, 768, 4096], P('outer', None, 'inner'), may hold values from -0.21875 to 0.21875
Outputs:
- mixed: bfloat16 [4096, 4096], P('outer', 'inner')
Inputs may be any that keep to these rules, and one draw needn't show every extreme that they name: `routes`: each row names 8 different experts; within each aligned block of 128 rows no expert is named more than 10 times, a bound that some block reaches.
All inputs are finite; a program needn't handle non-finite values.
Results may differ from a plain program's by a relative error of at most 0.024.
Values may be sent and summed in bfloat16 or wider, within the bound.
No kernel may reach another device: no remote copies, remote signals or barrier semaphores. Data moves between devices by JAX's collectives and lax.ppermute only.
A program may use at most 64 MiB of HBM per device.

v0:
```python
import jax
import jax.numpy as jnp
from jax import lax
from jax.sharding import PartitionSpec as P


def per_device(tokens, routes, gates, w_gate_up, w_down):
    row_count, feature_share = tokens.shape
    top_count = routes.shape[1]
    outer_count = lax.axis_size("outer")
    inner_count = lax.axis_size("inner")
    expert_group = w_gate_up.shape[0]
    experts = expert_group * outer_count
    capacity = max(2, 5 * row_count * top_count // (4 * experts))
    hidden_width = w_down.shape[1]
    hidden_share = hidden_width // inner_count
    flat_ids = routes.reshape(-1)
    onehot = (flat_ids[:, None] == jnp.arange(experts, dtype=jnp.int32)[None, :]).astype(jnp.int32)
    slot_rank = jnp.sum((jnp.cumsum(onehot, axis=0) - 1) * onehot, axis=1)
    target = flat_ids * capacity + slot_rank
    placing = jnp.arange(experts * capacity, dtype=jnp.int32)[:, None] == target[None, :]
    placing = jnp.sum(
        placing.reshape(experts * capacity, row_count, top_count).astype(jnp.bfloat16), axis=2
    )
    packed = jnp.dot(placing, tokens, preferred_element_type=jnp.float32).astype(jnp.bfloat16)
    packed = packed.reshape(outer_count, expert_group, capacity, feature_share)
    arrived = lax.all_to_all(packed, "outer", split_axis=0, concat_axis=0, tiled=True)
    slab = jnp.transpose(arrived, (1, 0, 2, 3)).reshape(
        expert_group, outer_count * capacity, feature_share
    )
    partial_value = jnp.einsum("erd,edh->erh", slab, w_gate_up, preferred_element_type=jnp.float32)
    slot_total = slab.shape[1]
    blocks = partial_value.reshape(expert_group, slot_total, inner_count, 2 * hidden_share)
    reduced = lax.psum_scatter(
        blocks.astype(jnp.bfloat16), "inner", scatter_dimension=2, tiled=True
    ).astype(jnp.float32)[:, :, 0]
    hidden = (jax.nn.silu(reduced[:, :, :hidden_share]) * reduced[:, :, hidden_share:]).astype(
        jnp.bfloat16
    )
    result = jnp.einsum(
        "erh,ehd->erd",
        lax.all_gather(hidden, "inner", axis=2, tiled=True),
        w_down,
        preferred_element_type=jnp.float32,
    )
    expert_out = result.astype(jnp.bfloat16).reshape(
        expert_group, outer_count, capacity, feature_share
    )
    expert_out = jnp.transpose(expert_out, (1, 0, 2, 3))
    home_rows = lax.all_to_all(
        expert_out, "outer", split_axis=0, concat_axis=0, tiled=True
    ).reshape(experts * capacity, feature_share)
    picked = home_rows[target].astype(jnp.float32).reshape(row_count, top_count, feature_share)
    mixed_out = tokens.astype(jnp.float32) + jnp.sum(gates[:, :, None] * picked, axis=1)
    return mixed_out.astype(jnp.bfloat16)


def solution(mesh):
    in_specs = (
        P("outer", "inner"),
        P("outer", None),
        P("outer", None),
        P("outer", "inner", None),
        P("outer", None, "inner"),
    )
    out_specs = P("outer", "inner")
    return jax.shard_map(
        per_device, mesh=mesh, in_specs=in_specs, out_specs=out_specs, check_vma=False
    )
```

profile of v0, /device:TPU:1, one launch (start us, length us, event | category | flops | bytes accessed | tf_op | source)
XLA Modules:
  0.0 316.9 jit_solution(3562367101690532886)
XLA Ops:
  6.5 0.9 copy.36
  8.0 0.8 copy-done.1
  8.8 1.1 add_add_fusion
  10.5 6.7 %fusion.1 = bf16[1280,128]{1,0:T(8,128)(2,1)S(1)} fusion(s32[128,8]{0,1:T(8,128)S(1)} %copy.41), kind=kLoop, calls=%fused_computation.4 | loop fusion | flops 3768320 | bytes 331776 | tf_op jit(solution)/shard_map/reduce_sum | solution.py:22
  17.3 1.2 convolution_convert_fusion.1
  18.4 2.1 reshape.85
  20.6 1.6 copy.42
  22.1 55.6 %all_to_all.10 = bf16[32,4,10,256]{3,1,2,0:T(4,128)(2,1)S(1)} all-to-all(bf16[32,4,10,256]{3,1,2,0:T(4,128)(2,1)S(1)} %copy.42), channel_id=1, replica_groups=mesh['outer'=32,'inner'=16] {'outer'}, dimensions={0} | all-to-all | bytes 1310720 | tf_op jit(solution)/shard_map/all_to_all | solution.py:27
  77.8 3.1 convolution_convert_fusion
  80.8 6.4 %copy.44 = bf16[4,320,1536]{1,2,0:T(8,128)(2,1)} copy(bf16[4,320,1536]{2,1,0:T(8,128)(2,1)} %convolution_convert_fusion) | data formatting | bytes 7864320 | tf_op jit(solution)/shard_map/convert_element_type | solution.py:35
  87.3 5.3 %copy.45 = bf16[4,320,16,96]{1,3,0,2:T(8,128)(2,1)} copy(bf16[4,320,16,96]{1,3,2,0:T(8,128)(2,1)} %bitcast.29) | data formatting | bytes 7864320 | tf_op jit(solution)/shard_map/convert_element_type | solution.py:35
  92.6 83.4 %reduce-scatter.4.cloned.1.call-done = bf16[4,320,1,96]{1,3,0,2:T(8,128)(2,1)} async-done(((bf16[4,320,16,96]{1,3,0,2:T(8,128)(2,1)}), bf16[4,320,1,96]{1,3,0,2:T(8,128)(2,1)}) %reduce-scatter.4.cloned.1.call-update) | async-done | bytes 245776
  176.0 1.0 bitcast_convert_fusion
  177.1 0.8 fusion.7
  177.8 62.6 %all-gather.2.cloned.1.call-done = bf16[4,320,768]{1,2,0:T(8,128)(2,1)} async-done(((bf16[4,320,48]{1,2,0:T(8,128)(2,1)}), bf16[4,320,768]{1,2,0:T(8,128)(2,1)}) %all-gather.2.cloned.1.call-update) | async-done | bytes 1966096 | tf_op jit(solution)/shard_map/all_gather | solution.py:42
  240.4 3.0 convolution_convert_fusion.2
  243.4 1.3 copy.46
  244.8 13.9 %all-to-all-start.1 = ((bf16[32,4,10,256]{3,1,2,0:T(4,128)(2,1)}), bf16[32,4,10,256]{3,1,2,0:T(4,128)(2,1)}, u32[]{:S(2)}, u32[]{:S(2)}) async-start(bf16[32,4,10,256]{3,1,2,0:T(4,128)(2,1)} %bitcast.31), calls=%async_computation.1 | async-start | bytes 1310720 | tf_op jit(solution)/shard_map/all_to_all | solution.py:50
  258.9 38.9 %all-to-all-done.1 = bf16[32,4,10,256]{3,1,2,0:T(4,128)(2,1)} async-done(((bf16[32,4,10,256]{3,1,2,0:T(4,128)(2,1)}), bf16[32,4,10,256]{3,1,2,0:T(4,128)(2,1)}, u32[]{:S(2)}, u32[]{:S(2)}) %all-to-all-start.1) | async-done | bytes 655392 | tf_op jit(solution)/shard_map/all_to_all | solution.py:50
  297.8 2.3 copy.47
  300.1 2.1 reshape.88
  302.2 5.7 %gather_fusion = bf16[1024,256]{1,0:T(8,128)(2,1)} fusion(bf16[1280,256]{1,0:T(8,128)(2,1)} %reshape.88, s32[1024]{0:T(1024)S(1)} %broadcast_clamp_fusion), kind=kCustom, calls=%fused_computation | custom fusion | bytes 1052672 | tf_op jit(solution)/shard_map/gather | solution.py:53
  307.9 1.4 fusion.2
  309.4 0.6 add_convert_fusion
  (27 shorter events, 1.4 us)
Async XLA Ops:
  6.5 71.2 %copy-start = (bf16[4,256,1536]{2,1,0:T(8,128)(2,1)S(1)}, bf16[4,256,1536]{2,1,0:T(8,128)(2,1)}, u32[]{:S(2)}) copy-start(bf16[4,256,1536]{2,1,0:T(8,128)(2,1)} %param.8) | copy-start | bytes 9437188
  6.5 10.7 %copy-start.2 = (bf16[128,256]{1,0:T(8,128)(2,1)S(1)}, bf16[128,256]{1,0:T(8,128)(2,1)}, u32[]{:S(2)}) copy-start(bf16[128,256]{1,0:T(8,128)(2,1)} %param.5) | copy-start | bytes 196612
  6.5 169.5 %reduce-scatter.4.cloned.1.call-start = ((), (), s32[]{:S(2)}) async-start(), calls=%async_computation.4 | async-start | bytes 5013504
  8.0 0.8 copy-start.1
  92.6 147.8 %all-gather.2.cloned.1.call-start = ((), (), s32[]{:S(2)}) async-start(), calls=%async_computation.3 | async-start | bytes 2506752 | tf_op jit(solution)/shard_map/all_gather | solution.py:42
  177.8 80.9 %copy-start.3 = (f32[128,8]{0,1:T(8,128)S(1)}, f32[128,8]{0,1:T(8,128)}, u32[]{:S(2)}) copy-start(f32[128,8]{0,1:T(8,128)} %param.7) | copy-start | bytes 12292
  244.8 53.1 %all-to-all-start.1 = ((bf16[32,4,10,256]{3,1,2,0:T(4,128)(2,1)}), bf16[32,4,10,256]{3,1,2,0:T(4,128)(2,1)}, u32[]{:S(2)}, u32[]{:S(2)}) async-start(bf16[32,4,10,256]{3,1,2,0:T(4,128)(2,1)} %bitcast.31), calls=%async_computation.1 | async-start | bytes 1310720 | tf_op jit(solution)/shard_map/all_to_all | solution.py:50
Sparse Core Ops, SparseCore 0:
  92.7 83.2 reduce-scatter.3
  179.1 61.2 all-gather.1
where the time goes:
time: 318 us; the launch traced here: 317 us
  waiting for transfers between devices  185 us (58%)
  blocking collectives  55.6 us (17%)
  local copies, waits for them, and re-layouts  29.3 us (9%)
  starting transfers between devices  14 us (4%)
  between operations  13.5 us (4%)
  other arithmetic  12.2 us (4%)
  matrix products  7.23 us (2%)
    unnamed x3, waiting for transfers between devices  83.4 us
    all_gather x1, waiting for transfers between devices, per_device(): lax.all_gather(hidden, 'inner', axis=2, tiled=True)  62.6 us
    all_to_all x1, blocking collectives, per_device(): lax.all_to_all(packed, 'outer', split_axis=0, concat_axis=0, tiled=True)  55.6 us
    all_to_all x1, waiting for transfers between devices, per_device(): lax.all_to_all(expert_out, 'outer', split_axis=0, concat_axis=0, tiled=True)  38.9 us
    all_to_all x1, starting transfers between devices, per_device(): lax.all_to_all(expert_out, 'outer', split_axis=0, concat_axis=0, tiled=True)  13.9 us
    convert_element_type x2, local copies, waits for them, and re-layouts, per_device(): blocks.astype(jnp.bfloat16)  11.7 us
    reduce_sum x1, other arithmetic, per_device(): jnp.sum(placing.reshape(experts * capacity, row_count, top_count).astype(...  6.71 us
  transfers between devices with their start and end apart: 3, of which 3 were waited for; matrix products, arithmetic and copies ran while one was open for 0% of the time, Pallas kernels for 0%

commit v1 on v0

v1 whole, which is shorter than its diff:
```python
import functools

import jax
import jax.numpy as jnp
from jax import lax
from jax.experimental import pallas as pl
from jax.experimental.pallas import tpu as pltpu
from jax.sharding import PartitionSpec as P

F32 = jnp.float32
BF16 = jnp.bfloat16
VMEM_LIMIT = 40 * 1024 * 1024


def iota(shape, dim):
    return lax.broadcasted_iota(jnp.int32, shape, dim)


def tenth(value):
    return (value * 6554) >> 16


def dot(a, b, contract=((1,), (0,))):
    return lax.dot_general(a, b, (contract, ((), ())), preferred_element_type=F32)


def slot_codes(routes_ref, experts):
    rows, top = routes_ref.shape
    expert = iota((rows, experts), 1)
    named = jnp.zeros((rows, experts), F32)
    for k in range(top):
        named = named + jnp.where(routes_ref[:, k : k + 1] == expert, 1.0, 0.0)
    earlier = jnp.where(iota((rows, rows), 1) < iota((rows, rows), 0), 1.0, 0.0).astype(BF16)
    rank = dot(earlier, named.astype(BF16))
    return (named * (rank + 1.0)).astype(BF16)


def pack_kernel(cap, experts, routes_ref, tokens_ref, packed_ref):
    rows = tokens_ref.shape[0]
    slots = experts * cap
    code = slot_codes(routes_ref, experts)
    slot = iota((slots, experts), 0)
    spread = jnp.where(tenth(slot) == iota((slots, experts), 1), 1.0, 0.0).astype(BF16)
    seen = dot(spread, code, ((1,), (1,)))
    slot = iota((slots, rows), 0)
    wanted = (slot - cap * tenth(slot) + 1).astype(F32)
    placing = jnp.where(seen == wanted, 1.0, 0.0).astype(BF16)
    packed_ref[...] = dot(placing, tokens_ref[...]).astype(BF16)


def gate_kernel(cap, experts, routes_ref, gates_ref, weights_ref):
    rows, top = routes_ref.shape
    slots = experts * cap
    code = slot_codes(routes_ref, experts)
    expert = iota((rows, experts), 1)
    gate = jnp.zeros((rows, experts), F32)
    for k in range(top):
        gate = gate + jnp.where(routes_ref[:, k : k + 1] == expert, gates_ref[:, k : k + 1], 0.0)
    slot = iota((experts, slots), 1)
    spread = jnp.where(tenth(slot) == iota((experts, slots), 0), 1.0, 0.0).astype(BF16)
    slot = iota((rows, slots), 1)
    mine = dot(code, spread) == (slot - cap * tenth(slot) + 1).astype(F32)
    for part in range(weights_ref.shape[0]):
        piece = gate.astype(BF16)
        gate = gate - piece.astype(F32)
        weights_ref[part] = jnp.where(mine, dot(piece, spread), 0.0).astype(BF16)


def pair_slots(cap, group, per_expert, pair, shape, dim):
    lane = iota(shape, dim)
    second = jnp.where(lane >= per_expert, 1, 0)
    lane = lane - per_expert * second
    source = tenth(lane)
    return source * (group * cap) + (2 * pair + second) * cap + (lane - cap * source)


def up_kernel(cap, group, per_expert, arrived_ref, w_ref, out_ref, slab_ref):
    pair, column = pl.program_id(0), pl.program_id(1)
    slots = arrived_ref.shape[0]
    both = 2 * per_expert
    mid = per_expert // 128 * 128

    @pl.when(column == 0)
    def _():
        source = pair_slots(cap, group, per_expert, pair, (both, slots), 0)
        order = jnp.where(source == iota((both, slots), 1), 1.0, 0.0).astype(BF16)
        slab_ref[...] = dot(order, arrived_ref[...]).astype(BF16)

    first = dot(w_ref[0], slab_ref[: mid + 128, :], ((0,), (1,)))
    second = dot(w_ref[1], slab_ref[mid:, :], ((0,), (1,)))
    lane = iota((first.shape[0], 128), 1)
    out_ref[:, :mid] = first[:, :mid].astype(BF16)
    out_ref[:, mid : mid + 128] = jnp.where(
        lane < per_expert - mid, first[:, mid:], second[:, :128]
    ).astype(BF16)
    out_ref[:, mid + 128 :] = second[:, 128:].astype(BF16)


def sum_kernel(parts_ref, out_ref):
    total = parts_ref[0].astype(F32)
    for n in range(1, parts_ref.shape[0]):
        total = total + parts_ref[n].astype(F32)
    out_ref[...] = total.astype(BF16)


def hidden_kernel(parts_ref, out_ref):
    total = parts_ref[0].astype(F32)
    for n in range(1, parts_ref.shape[0]):
        total = total + parts_ref[n].astype(F32)
    share = total.shape[0] // 2
    gate, up = total[:share], total[share:]
    hidden = (gate / (1.0 + jnp.exp(-gate)) * up).astype(BF16)
    for n in range(out_ref.shape[0]):
        out_ref[n] = hidden


def down_kernel(cap, group, per_expert, hidden_ref, w_ref, out_ref, total_ref):
    pair = pl.program_id(0)
    slots = out_ref.shape[0]
    both = 2 * per_expert
    mid = per_expert // 128 * 128
    first = dot(hidden_ref[:, : mid + 128], w_ref[0], ((0,), (0,))).astype(BF16)
    second = dot(hidden_ref[:, mid:], w_ref[1], ((0,), (0,))).astype(BF16)
    rows = jnp.concatenate([first[:per_expert], second[per_expert - mid :]], axis=0)
    source = pair_slots(cap, group, per_expert, pair, (slots, both), 1)
    order = jnp.where(source == iota((slots, both), 0), 1.0, 0.0).astype(BF16)
    placed = dot(order, rows)

    @pl.when(pair == 0)
    def _():
        total_ref[...] = placed

    @pl.when(pair == pl.num_programs(0) - 1)
    def _():
        out_ref[...] = (total_ref[...] + placed).astype(BF16)


def mix_kernel(tokens_ref, weights_ref, home_ref, out_ref):
    total = tokens_ref[...].astype(F32)
    home = home_ref[...]
    for part in range(weights_ref.shape[0]):
        total = total + dot(weights_ref[part], home)
    out_ref[...] = total.astype(BF16)


def params(*semantics):
    return pltpu.CompilerParams(
        dimension_semantics=semantics or None, vmem_limit_bytes=VMEM_LIMIT
    )


def cost(flops, nbytes):
    return pl.CostEstimate(flops=flops, bytes_accessed=nbytes, transcendentals=0)


def groups_of(outer, side):
    along, across, whole = [], [], []
    for o in range(outer):
        square = [[o * side * side + y * side + x for x in range(side)] for y in range(side)]
        turned = [list(line) for line in zip(*square)]
        if o % 2 == 0:
            square, turned = turned, square
        along += turned
        across += square
        whole.append([device for line in square for device in line])
    return along, across, whole


def per_device(mesh_shape, tokens, routes, gates, w_gate_up, w_down):
    rows, features = tokens.shape
    outer, inner = mesh_shape
    group, _, columns = w_gate_up.shape
    hidden = w_down.shape[1]
    experts = group * outer
    cap = 10
    slots = experts * cap
    per_expert = outer * cap
    side = 4
    axes = ("outer", "inner")
    along, across, whole = groups_of(outer, side)

    packed = pl.pallas_call(
        functools.partial(pack_kernel, cap, experts),
        out_shape=jax.ShapeDtypeStruct((slots, features), BF16),
        compiler_params=params(),
        cost_estimate=cost(2 * slots * rows * 384, 2 * slots * features),
        name="pack",
    )(routes, tokens)
    arrived = lax.all_to_all(packed, "outer", split_axis=0, concat_axis=0, tiled=True)

    tile = columns // side
    partial_value = pl.pallas_call(
        functools.partial(up_kernel, cap, group, per_expert),
        grid=(group // 2, columns // tile),
        in_specs=[
            pl.BlockSpec((slots, features), lambda p, c: (0, 0)),
            pl.BlockSpec((2, features, tile), lambda p, c: (p, 0, c)),
        ],
        out_specs=pl.BlockSpec((tile, 2 * per_expert), lambda p, c: (c, p)),
        out_shape=jax.ShapeDtypeStruct((columns, slots), BF16),
        scratch_shapes=[pltpu.VMEM((2 * per_expert, features), BF16)],
        compiler_params=params("arbitrary", "arbitrary"),
        cost_estimate=cost(2 * slots * features * (columns + slots), 2 * columns * slots),
        name="gate_up",
    )(arrived, w_gate_up)

    swapped = lax.all_to_all(
        partial_value, axes, split_axis=0, concat_axis=0, tiled=True, axis_index_groups=along
    )
    quarter = columns // side
    lanes = 256
    summed = pl.pallas_call(
        sum_kernel,
        grid=(slots // lanes,),
        in_specs=[pl.BlockSpec((side, quarter, lanes), lambda n: (0, 0, n))],
        out_specs=pl.BlockSpec((quarter, lanes), lambda n: (0, n)),
        out_shape=jax.ShapeDtypeStruct((quarter, slots), BF16),
        compiler_params=params("arbitrary"),
        cost_estimate=cost(columns * slots, 2 * columns * slots),
        name="first_sum",
    )(swapped.reshape(side, quarter, slots))
    swapped = lax.all_to_all(
        summed, axes, split_axis=0, concat_axis=0, tiled=True, axis_index_groups=across
    )
    share = columns // inner
    mine = pl.pallas_call(
        hidden_kernel,
        grid=(slots // lanes,),
        in_specs=[pl.BlockSpec((side, share, lanes), lambda n: (0, 0, n))],
        out_specs=pl.BlockSpec((inner, share // 2, lanes), lambda n: (0, 0, n)),
        out_shape=jax.ShapeDtypeStruct((inner, share // 2, slots), BF16),
        compiler_params=params("arbitrary"),
        cost_estimate=cost(quarter * slots, 4 * quarter * slots),
        name="hidden",
    )(swapped.reshape(side, share, slots))
    gathered = lax.all_to_all(
        mine.reshape(hidden, slots),
        axes,
        split_axis=0,
        concat_axis=0,
        tiled=True,
        axis_index_groups=whole,
    )
    expert_out = pl.pallas_call(
        functools.partial(down_kernel, cap, group, per_expert),
        grid=(group // 2,),
        in_specs=[
            pl.BlockSpec((hidden, 2 * per_expert), lambda p: (0, p)),
            pl.BlockSpec((2, hidden, features), lambda p: (p, 0, 0)),
        ],
        out_specs=pl.BlockSpec((slots, features), lambda p: (0, 0)),
        out_shape=jax.ShapeDtypeStruct((slots, features), BF16),
        scratch_shapes=[pltpu.VMEM((slots, features), F32)],
        compiler_params=params("arbitrary"),
        cost_estimate=cost(2 * slots * features * (hidden + slots), 4 * hidden * slots),
        name="down",
    )(gathered, w_down)
    weights = pl.pallas_call(
        functools.partial(gate_kernel, cap, experts),
        out_shape=jax.ShapeDtypeStruct((3, rows, slots), BF16),
        compiler_params=params(),
        cost_estimate=cost(8 * rows * experts * slots, 6 * rows * slots),
        name="gate_weights",
    )(routes, gates)
    home = lax.all_to_all(expert_out, "outer", split_axis=0, concat_axis=0, tiled=True)
    return pl.pallas_call(
        mix_kernel,
        out_shape=jax.ShapeDtypeStruct((rows, features), BF16),
        compiler_params=params(),
        cost_estimate=cost(6 * rows * slots * features, 2 * slots * features),
        name="mix",
    )(tokens, weights, home)


def solution(mesh):
    in_specs = (
        P("outer", "inner"),
        P("outer", None),
        P("outer", None),
        P("outer", "inner", None),
        P("outer", None, "inner"),
    )
    return jax.shard_map(
        functools.partial(per_device, (mesh.shape["outer"], mesh.shape["inner"])),
        mesh=mesh,
        in_specs=in_specs,
        out_specs=P("outer", "inner"),
        check_vma=False,
    )
```

time: 318 us -> 187 us (0.59)
  waiting for transfers between devices: 185 us -> 38.1 us
  blocking collectives: 55.6 us -> 125 us
  local copies, waits for them, and re-layouts: 29.3 us -> 3.62 us
  between operations: 13.5 us -> 0.06 us
  Pallas kernels: 0 us -> 13 us
  other arithmetic: 12.2 us -> 0 us
  matrix products: 7.23 us -> 0 us
  starting transfers between devices: 14 us -> 7.5 us
    unnamed x3 -> x0, waiting for transfers between devices: 83.4 us -> none
    all_to_all x0 -> x3, blocking collectives: none -> 69 us  [the longest x1 29.2 us: per_device(): lax.all_to_all(partial_value, axes, split_axis=0, concat_axis=0, tiled=Tr...]
    all_gather x1 -> x0, waiting for transfers between devices: 62.6 us -> none  [per_device(): lax.all_gather(hidden, 'inner', axis=2, tiled=True)]
    convert_element_type x3 -> x0, local copies, waits for them, and re-layouts: 13.1 us -> none  [the longest x2 11.7 us: per_device(): blocks.astype(jnp.bfloat16)]
    pallas_call x0 -> x7, Pallas kernels: none -> 13 us  [the longest x1 5.13 us: per_device(): pl.pallas_call(functools.partial(up_kernel, cap, group, per_expert), grid...]
    reduce_sum x3 -> x0, other arithmetic: 8.49 us -> none  [the longest x1 6.71 us: per_device(): jnp.sum(placing.reshape(experts * capacity, row_count, top_count).astype(...]
    dot_general x3 -> x0, matrix products: 7.23 us -> none  [the longest x1 3.08 us: per_device(): jnp.einsum('erd,edh->erh', slab, w_gate_up, preferred_element_type=jnp.fl...]
    all_to_all x1, starting transfers between devices: 13.9 us -> 7.5 us  [per_device(): lax.all_to_all(expert_out, 'outer', split_axis=0, concat_axis=0, tiled=True)]
  transfers between devices with their start and end apart: 3 -> 1, of which waited for: 3 -> 1; matrix products, arithmetic and copies ran while one was open for 0% -> 0% of each run, Pallas kernels for 0% -> 0%
where the time goes in v1:
time: 187 us
  blocking collectives  125 us (67%)
  waiting for transfers between devices  38.1 us (20%)
  Pallas kernels  13 us (7%)
  starting transfers between devices  7.5 us (4%)
  local copies, waits for them, and re-layouts  3.62 us (2%)
    all_to_all x1, blocking collectives, per_device(): lax.all_to_all(packed, 'outer', split_axis=0, concat_axis=0, tiled=True)  55.6 us
    all_to_all x1, waiting for transfers between devices, per_device(): lax.all_to_all(expert_out, 'outer', split_axis=0, concat_axis=0, tiled=True)  38.1 us
    all_to_all x1, blocking collectives, per_device(): lax.all_to_all(partial_value, axes, split_axis=0, concat_axis=0, tiled=Tr...  29.2 us
    all_to_all x1, blocking collectives, per_device(): lax.all_to_all(mine.reshape(hidden, slots), axes, split_axis=0, concat_ax...  26.4 us
    all_to_all x1, blocking collectives, per_device(): lax.all_to_all(summed, axes, split_axis=0, concat_axis=0, tiled=True, axi...  13.5 us
    all_to_all x1, starting transfers between devices, per_device(): lax.all_to_all(expert_out, 'outer', split_axis=0, concat_axis=0, tiled=True)  7.5 us
    pallas_call x1, Pallas kernels, per_device(): pl.pallas_call(functools.partial(up_kernel, cap, group, per_expert), grid...  5.13 us
  transfers between devices with their start and end apart: 1, of which 1 were waited for; matrix products, arithmetic and copies ran while one was open for 0% of the time, Pallas kernels for 0%

profile of v1, /device:TPU:1, one launch (start us, length us, event | category | flops | bytes accessed | tf_op | source)
XLA Modules:
  0.0 186.9 jit_solution(14133679156215225210)
XLA Ops:
  0.0 0.8 copy.6.routes_ref
  0.8 0.0 copy-start.1
  0.8 0.8 copy-done.1
  1.6 0.9 pack.1
  2.6 55.6 %all_to_all.48 = bf16[32,40,256]{2,1,0:T(8,128)(2,1)S(1)} all-to-all(bf16[32,40,256]{2,1,0:T(8,128)(2,1)S(1)} %bitcast.10), channel_id=1, replica_groups=mesh['outer'=32,'inner'=16] {'outer'}, dimensions={0} | all-to-all | bytes 1310720 | tf_op jit(solution)/shard_map/all_to_all | solution.py:189
  58.2 0.0 copy-start
  58.2 1.9 %copy-done = bf16[4,256,1536]{2,1,0:T(8,128)(2,1)S(1)} copy-done((bf16[4,256,1536]{2,1,0:T(8,128)(2,1)S(1)}, bf16[4,256,1536]{2,1,0:T(8,128)(2,1)}, u32[]{:S(2)}) %copy-start) | copy-done | bytes 3145752
  60.1 5.1 %gate_up.1 = bf16[1536,1280]{1,0:T(8,128)(2,1)S(1)} custom-call(bf16[1280,256]{1,0:T(8,128)(2,1)S(1)} %bitcast.11, bf16[4,256,1536]{2,1,0:T(8,128)(2,1)S(1)} %copy-done), custom_call_target="tpu_custom_call" | custom-call | flops 1845493760 | bytes 3932160 | tf_op jit(solution)/shard_map/gate_up/pallas_call | solution.py:192
  65.2 29.2 %all_to_all.49.parts_ref = bf16[4,384,1280]{2,1,0:T(8,128)(2,1)S(1)} all-to-all(bf16[4,384,1280]{2,1,0:T(8,128)(2,1)S(1)} %bitcast.7), channel_id=1, replica_groups={{0,1,2,3},{4,5,6,7},{8,9,10,11},{12,13,14,15},{16,20,24,28},{17,21,25,2..., dimensions={0} | all-to-all | bytes 7864320 | tf_op jit(solution)/shard_map/all_to_all | solution.py:207
  94.4 0.9 first_sum.1
  95.3 13.5 %all_to_all.50.parts_ref = bf16[4,96,1280]{2,1,0:T(8,128)(2,1)S(1)} all-to-all(bf16[4,96,1280]{2,1,0:T(8,128)(2,1)S(1)} %bitcast.8), channel_id=1, replica_groups={{0,4,8,12},{1,5,9,13},{2,6,10,14},{3,7,11,15},{16,17,18,19},{20,21,22,2..., dimensions={0} | all-to-all | bytes 1966080 | tf_op jit(solution)/shard_map/all_to_all | solution.py:222
  108.8 0.6 hidden.1
  109.4 26.4 %all_to_all.51 = bf16[16,48,1280]{2,1,0:T(8,128)(2,1)S(1)} all-to-all(bf16[16,48,1280]{2,1,0:T(8,128)(2,1)S(1)} %hidden.1), channel_id=1, replica_groups={{0,4,8,12,1,5,9,13,2,6,10,14,3,7,11,15},{16,17,18,19,20,21,22,23,24,25,..., dimensions={0} | all-to-all | bytes 3932160 | tf_op jit(solution)/shard_map/all_to_all | solution.py:236
  135.7 0.0 copy-start.4
  135.7 0.0 copy-done.3
  135.7 0.0 copy-start.2
  135.7 3.5 %down.1 = bf16[1280,256]{1,0:T(8,128)(2,1)} custom-call(bf16[768,1280]{1,0:T(8,128)(2,1)S(1)} %bitcast.12, bf16[4,768,256]{2,1,0:T(8,128)(2,1)S(1)} %copy-done.3), custom_call_target="tpu_custom_call" | custom-call | flops 1342177280 | bytes 3932160 | tf_op jit(solution)/shard_map/down/pallas_call | solution.py:244
  139.2 7.5 %all-to-all-start.4 = ((bf16[32,40,256]{2,1,0:T(8,128)(2,1)}), bf16[32,40,256]{2,1,0:T(8,128)(2,1)S(1)}, u32[]{:S(2)}, u32[]{:S(2)}) async-start(bf16[32,40,256]{2,1,0:T(8,128)(2,1)} %bitcast.5), calls=%async_computation.4 | async-start | bytes 1310720 | tf_op jit(solution)/shard_map/all_to_all | solution.py:265
  146.7 0.0 copy-done.4
  146.8 0.1 copy.7.gates_ref
  146.9 0.9 gate_weights.1.weights_ref
  147.7 38.1 %all-to-all-done.4 = bf16[32,40,256]{2,1,0:T(8,128)(2,1)S(1)} async-done(((bf16[32,40,256]{2,1,0:T(8,128)(2,1)}), bf16[32,40,256]{2,1,0:T(8,128)(2,1)S(1)}, u32[]{:S(2)}, u32[]{:S(2)}) %all-to-all-start.4) | async-done | bytes 655392 | tf_op jit(solution)/shard_map/all_to_all | solution.py:265
  185.8 0.0 copy-done.2
  185.8 1.1 mix.1
  (1 shorter events, 0.0 us)
Async XLA Ops:
  0.8 0.8 copy-start.1
  58.2 1.9 %copy-start = (bf16[4,256,1536]{2,1,0:T(8,128)(2,1)S(1)}, bf16[4,256,1536]{2,1,0:T(8,128)(2,1)}, u32[]{:S(2)}) copy-start(bf16[4,256,1536]{2,1,0:T(8,128)(2,1)} %w_ref.2) | copy-start | bytes 9437188
  108.8 26.9 %copy-start.3 = (bf16[4,768,256]{2,1,0:T(8,128)(2,1)S(1)}, bf16[4,768,256]{2,1,0:T(8,128)(2,1)}, u32[]{:S(2)}) copy-start(bf16[4,768,256]{2,1,0:T(8,128)(2,1)} %w_ref.3) | copy-start | bytes 4718596
  135.7 11.0 %copy-start.4 = (f32[128,8]{0,1:T(8,128)S(1)}, f32[128,8]{0,1:T(8,128)}, u32[]{:S(2)}) copy-start(f32[128,8]{0,1:T(8,128)} %param.7) | copy-start | bytes 12292
  135.7 50.1 %copy-start.2 = (bf16[128,256]{1,0:T(8,128)(2,1)S(1)}, bf16[128,256]{1,0:T(8,128)(2,1)}, u32[]{:S(2)}) copy-start(bf16[128,256]{1,0:T(8,128)(2,1)} %tokens_ref.3) | copy-start | bytes 196612
  139.2 46.6 %all-to-all-start.4 = ((bf16[32,40,256]{2,1,0:T(8,128)(2,1)}), bf16[32,40,256]{2,1,0:T(8,128)(2,1)S(1)}, u32[]{:S(2)}, u32[]{:S(2)}) async-start(bf16[32,40,256]{2,1,0:T(8,128)(2,1)} %bitcast.5), calls=%async_computation.4 | async-start | bytes 1310720 | tf_op jit(solution)/shard_map/all_to_all | solution.py:265

commit v2 on v0

v2 whole, which is shorter than its diff:
```python
import functools

import jax
import jax.numpy as jnp
from jax import lax
from jax.experimental import pallas as pl
from jax.experimental.pallas import tpu as pltpu
from jax.sharding import PartitionSpec as P

F32 = jnp.float32
BF16 = jnp.bfloat16
VMEM_LIMIT = 40 * 1024 * 1024


def iota(shape, dim):
    return lax.broadcasted_iota(jnp.int32, shape, dim)


def tenth(value):
    return (value * 6554) >> 16


def dot(a, b, contract=((1,), (0,))):
    return lax.dot_general(a, b, (contract, ((), ())), preferred_element_type=F32)


def slot_codes(named):
    rows = named.shape[1]
    earlier = jnp.where(iota((rows, rows), 0) < iota((rows, rows), 1), 1.0, 0.0).astype(BF16)
    rank = dot(named.astype(BF16), earlier)
    return named * (rank + 1.0)


def pack_kernel(cap, experts, routes_ref, tokens_ref, packed_ref):
    top, rows = routes_ref.shape
    slots = experts * cap
    expert = iota((experts, rows), 0)
    named = jnp.zeros((experts, rows), F32)
    for k in range(top):
        named = named + jnp.where(routes_ref[k : k + 1, :] == expert, 1.0, 0.0)
    code = slot_codes(named).astype(BF16)
    slot = iota((slots, 1), 0)
    spread = jnp.where(tenth(slot) == iota((slots, experts), 1), 1.0, 0.0).astype(BF16)
    wanted = (slot - cap * tenth(slot) + 1).astype(F32)
    placing = jnp.where(dot(spread, code) == wanted, 1.0, 0.0).astype(BF16)
    packed_ref[...] = dot(placing, tokens_ref[...]).astype(BF16)


def gate_kernel(cap, experts, routes_ref, gates_ref, weights_ref):
    top, rows = routes_ref.shape
    slots = experts * cap
    expert = iota((experts, rows), 0)
    named = jnp.zeros((experts, rows), F32)
    gate = jnp.zeros((experts, rows), F32)
    for k in range(top):
        here = routes_ref[k : k + 1, :] == expert
        named = named + jnp.where(here, 1.0, 0.0)
        gate = gate + jnp.where(here, gates_ref[k : k + 1, :], 0.0)
    code = slot_codes(named).T.astype(BF16)
    gate = gate.T
    slot = iota((1, slots), 1)
    spread = jnp.where(tenth(slot) == iota((experts, slots), 0), 1.0, 0.0).astype(BF16)
    mine = dot(code, spread) == (slot - cap * tenth(slot) + 1).astype(F32)
    for part in range(weights_ref.shape[0]):
        piece = gate.astype(BF16)
        gate = gate - piece.astype(F32)
        weights_ref[part] = jnp.where(mine, dot(piece, spread), 0.0).astype(BF16)


def expert_order(cap, group, sources, shape, dim):
    row = iota(shape, dim)
    piece = tenth(row)
    expert = jnp.zeros_like(piece)
    for n in range(1, group):
        expert = expert + jnp.where(piece >= n * sources, 1, 0)
    source = piece - sources * expert
    return source * (group * cap) + expert * cap + (row - cap * piece)


def to_experts_kernel(cap, group, sources, rows_ref, out_ref):
    batch = sources * group * cap
    each = sources * cap
    place = expert_order(cap, group, sources, (batch, 1), 0)
    order = jnp.where(place == iota((batch, batch), 1), 1.0, 0.0).astype(BF16)
    for n in range(rows_ref.shape[0] // batch):
        moved = dot(order, rows_ref[n * batch : (n + 1) * batch, :]).astype(BF16)
        for e in range(group):
            out_ref[e, n * each : (n + 1) * each, :] = moved[e * each : (e + 1) * each]


def to_sources_kernel(cap, group, sources, rows_ref, out_ref):
    batch = sources * group * cap
    each = sources * cap
    place = expert_order(cap, group, sources, (1, batch), 1)
    order = jnp.where(place == iota((batch, batch), 0), 1.0, 0.0).astype(BF16)
    for n in range(out_ref.shape[0] // batch):
        rows = jnp.concatenate(
            [rows_ref[e, n * each : (n + 1) * each, :] for e in range(group)], axis=0
        )
        out_ref[n * batch : (n + 1) * batch, :] = dot(order, rows).astype(BF16)


def up_kernel(me_ref, rows_ref, own_ref, *refs):
    others, out_ref = refs[:-1], refs[-1]
    side = rows_ref.shape[0]
    tile = out_ref.shape[2]
    total = dot(rows_ref[me_ref[0]], own_ref[0])
    for k, w_ref in enumerate(others, 1):
        total = total + dot(rows_ref[lax.rem(me_ref[0] + side - k, side)], w_ref[...])
    for n in range(out_ref.shape[0]):
        out_ref[n] = total[:, n * tile : (n + 1) * tile].astype(BF16)


def hidden_kernel(share, parts_ref, out_ref):
    total = parts_ref[0].astype(F32)
    for n in range(1, parts_ref.shape[0]):
        total = total + parts_ref[n].astype(F32)
    width = total.shape[1]
    up = pltpu.roll(total, width - share, 1)
    mixed = (total / (1.0 + jnp.exp(-total)) * up).astype(BF16)
    column = iota((width, 1), 0)
    block = jnp.zeros_like(column)
    for n in range(1, width // (2 * share)):
        block = block + jnp.where(column >= 2 * share * n, 1, 0)
    unit = jnp.where(column - 2 * share * block < share, column - share * block, -width)
    lane = iota((width, width), 1)
    left = jnp.where(unit == lane, 1.0, 0.0).astype(BF16)
    right = jnp.where(unit + width // 2 == lane, 1.0, 0.0).astype(BF16)
    half = total.shape[0] // 2
    hidden = (dot(mixed[:half], left) + dot(mixed[half:], right)).astype(BF16)
    for n in range(out_ref.shape[0]):
        out_ref[n] = hidden


def down_kernel(batches, me_ref, hidden_ref, own_ref, *refs):
    others, out_ref = refs[:-1], refs[-1]
    side, packed, width = hidden_ref.shape
    half = packed // batches
    left = jnp.concatenate([hidden_ref[b, :, : width // 2] for b in range(side)], axis=1)
    right = jnp.concatenate([hidden_ref[b, :, width // 2 :] for b in range(side)], axis=1)
    pieces = []
    for n in range(batches):
        pieces += [left[n * half : (n + 1) * half], right[n * half : (n + 1) * half]]
    hidden = jnp.concatenate(pieces, axis=0)
    out_ref[me_ref[0]] = dot(hidden, own_ref[0]).astype(BF16)
    features = out_ref.shape[2]
    for k, w_ref in enumerate(others, 1):
        depth = w_ref.shape[0]
        total = None
        for n in range(hidden.shape[1] // depth):
            w = w_ref[:, n * features : (n + 1) * features]
            term = dot(hidden[:, n * depth : (n + 1) * depth], w)
            total = term if total is None else total + term
        out_ref[lax.rem(me_ref[0] + side - k, side)] = total.astype(BF16)


def mix_kernel(tokens_ref, weights_ref, home_ref, out_ref):
    total = tokens_ref[...].astype(F32)
    home = home_ref[...]
    for part in range(weights_ref.shape[0]):
        total = total + dot(weights_ref[part], home)
    out_ref[...] = total.astype(BF16)


def params(*semantics):
    return pltpu.CompilerParams(
        dimension_semantics=semantics or None, vmem_limit_bytes=VMEM_LIMIT
    )


def cost(flops, nbytes):
    return pl.CostEstimate(flops=flops, bytes_accessed=nbytes, transcendentals=0)


def lines_of(outer, side):
    along, across = [], []
    for o in range(outer):
        rows = [[o * side * side + y * side + x for x in range(side)] for y in range(side)]
        columns = [list(line) for line in zip(*rows)]
        along += columns if o % 2 == 0 else rows
        across += rows if o % 2 == 0 else columns
    return along, across


def per_device(mesh_shape, tokens, routes, gates, w_gate_up, w_down):
    rows, features = tokens.shape
    outer, inner = mesh_shape
    group, _, columns = w_gate_up.shape
    hidden = w_down.shape[1]
    experts = group * outer
    cap = 10
    slots = experts * cap
    per_expert = outer * cap
    side = group
    sources = 8
    axes = ("outer", "inner")
    along, across = lines_of(outer, side)
    square = lax.axis_index("inner")
    me = jnp.where(lax.axis_index("outer") % 2 == 0, square // side, square % side)
    me_ref = me.astype(jnp.int32).reshape(1)

    def exchange(value, lines):
        return lax.all_to_all(
            value, axes, split_axis=0, concat_axis=0, tiled=True, axis_index_groups=lines
        )

    def take(weights, k):
        return lax.dynamic_index_in_dim(weights, (me + k) % side, 0, keepdims=False)

    line_weights = []
    for k in range(1, side):
        pairs = [(line[n], line[(n + k) % side]) for line in along for n in range(side)]
        down = take(w_down, k)
        blocks = [down[n : n + features] for n in range(0, hidden, features)]
        moved = jnp.concatenate([take(w_gate_up, k), *blocks], axis=1)
        line_weights.append(lax.ppermute(moved, axes, pairs))
    routes, gates = routes.T, gates.T

    packed = pl.pallas_call(
        functools.partial(pack_kernel, cap, experts),
        out_shape=jax.ShapeDtypeStruct((slots, features), BF16),
        compiler_params=params(),
        cost_estimate=cost(2 * slots * rows * 384, 2 * slots * features),
        name="pack",
    )(routes, tokens)
    arrived = lax.all_to_all(packed, "outer", split_axis=0, concat_axis=0, tiled=True)
    by_expert = pl.pallas_call(
        functools.partial(to_experts_kernel, cap, group, sources),
        out_shape=jax.ShapeDtypeStruct((group, per_expert, features), BF16),
        compiler_params=params(),
        cost_estimate=cost(2 * slots * features * 320, 4 * slots * features),
        name="to_experts",
    )(arrived)
    by_expert = exchange(by_expert.reshape(slots, features), along)

    tile = columns // side
    partial_value = pl.pallas_call(
        up_kernel,
        grid_spec=pltpu.PrefetchScalarGridSpec(
            num_scalar_prefetch=1,
            grid=(side // 2,),
            in_specs=[
                pl.BlockSpec((side, per_expert, features), lambda c, me: (0, 0, 0)),
                pl.BlockSpec((1, features, 2 * tile), lambda c, me: (me[0], 0, c)),
            ]
            + [pl.BlockSpec((features, 2 * tile), lambda c, me: (0, c))] * (side - 1),
            out_specs=pl.BlockSpec((2, per_expert, tile), lambda c, me: (c, 0, 0)),
        ),
        out_shape=jax.ShapeDtypeStruct((side, per_expert, tile), BF16),
        compiler_params=params("arbitrary"),
        cost_estimate=cost(2 * slots * features * columns, 8 * features * columns),
        name="gate_up",
    )(me_ref, by_expert.reshape(side, per_expert, features), w_gate_up, *line_weights)
    swapped = exchange(partial_value.reshape(side * per_expert, tile), across)
    batches = 2
    packed_rows = per_expert // 2
    mine = pl.pallas_call(
        functools.partial(hidden_kernel, hidden // inner),
        grid=(batches,),
        in_specs=[pl.BlockSpec((side, per_expert // batches, tile), lambda n: (0, n, 0))],
        out_specs=pl.BlockSpec((side, packed_rows // batches, tile), lambda n: (0, n, 0)),
        out_shape=jax.ShapeDtypeStruct((side, packed_rows, tile), BF16),
        compiler_params=params("arbitrary"),
        cost_estimate=cost(per_expert * tile * tile, 4 * per_expert * tile * side),
        name="hidden",
    )(swapped.reshape(side, per_expert, tile))
    gathered = exchange(mine.reshape(side * packed_rows, tile), across)
    expert_out = pl.pallas_call(
        functools.partial(down_kernel, batches),
        grid_spec=pltpu.PrefetchScalarGridSpec(
            num_scalar_prefetch=1,
            grid=(1,),
            in_specs=[
                pl.BlockSpec((side, packed_rows, tile), lambda n, me: (0, 0, 0)),
                pl.BlockSpec((1, hidden, features), lambda n, me: (me[0], 0, 0)),
            ]
            + [pl.BlockSpec((features, hidden), lambda n, me: (0, columns // hidden))] * (side - 1),
            out_specs=pl.BlockSpec((side, per_expert, features), lambda n, me: (0, 0, 0)),
        ),
        out_shape=jax.ShapeDtypeStruct((side, per_expert, features), BF16),
        compiler_params=params("arbitrary"),
        cost_estimate=cost(2 * slots * features * hidden, 8 * features * hidden),
        name="down",
    )(me_ref, gathered.reshape(side, packed_rows, tile), w_down, *line_weights)
    returned = exchange(expert_out.reshape(slots, features), along)
    by_source = pl.pallas_call(
        functools.partial(to_sources_kernel, cap, group, sources),
        out_shape=jax.ShapeDtypeStruct((slots, features), BF16),
        compiler_params=params(),
        cost_estimate=cost(2 * slots * features * 320, 4 * slots * features),
        name="to_sources",
    )(returned.reshape(group, per_expert, features))
    weights = pl.pallas_call(
        functools.partial(gate_kernel, cap, experts),
        out_shape=jax.ShapeDtypeStruct((3, rows, slots), BF16),
        compiler_params=params(),
        cost_estimate=cost(8 * rows * experts * slots, 6 * rows * slots),
        name="gate_weights",
    )(routes, gates)
    home = lax.all_to_all(by_source, "outer", split_axis=0, concat_axis=0, tiled=True)
    return pl.pallas_call(
        mix_kernel,
        out_shape=jax.ShapeDtypeStruct((rows, features), BF16),
        compiler_params=params(),
        cost_estimate=cost(6 * rows * slots * features, 2 * slots * features),
        name="mix",
    )(tokens, weights, home)


def solution(mesh):
    in_specs = (
        P("outer", "inner"),
        P("outer", None),
        P("outer", None),
        P("outer", "inner", None),
        P("outer", None, "inner"),
    )
    return jax.shard_map(
        functools.partial(per_device, (mesh.shape["outer"], mesh.shape["inner"])),
        mesh=mesh,
        in_specs=in_specs,
        out_specs=P("outer", "inner"),
        check_vma=False,
    )
```

time: 318 us -> 164 us (0.52)
  waiting for transfers between devices: 185 us -> 71.1 us
  starting transfers between devices: 14 us -> 39.1 us
  local copies, waits for them, and re-layouts: 29.3 us -> 5.08 us
  blocking collectives: 55.6 us -> 32.8 us
  between operations: 13.5 us -> 0.3 us
  Pallas kernels: 0 us -> 11.1 us
  other arithmetic: 12.2 us -> 3.34 us
  matrix products: 7.23 us -> 0 us
    unnamed x3 -> x0, waiting for transfers between devices: 83.4 us -> none
    all_gather x1 -> x0, waiting for transfers between devices: 62.6 us -> none  [per_device(): lax.all_gather(hidden, 'inner', axis=2, tiled=True)]
    all_to_all x1 -> x3, waiting for transfers between devices: 38.9 us -> 71.1 us  [the longest x1 38.3 us: per_device(): lax.all_to_all(by_source, 'outer', split_axis=0, concat_axis=0, tiled=True)]
    all_to_all x1 -> x3, blocking collectives: 55.6 us -> 32.8 us  [exchange(): lax.all_to_all(value, axes, split_axis=0, concat_axis=0, tiled=True, axis...]
    all_to_all x1 -> x3, starting transfers between devices: 13.9 us -> 29.8 us  [the longest x1 16.8 us: per_device(): lax.all_to_all(packed, 'outer', split_axis=0, concat_axis=0, tiled=True)]
    convert_element_type x3 -> x0, local copies, waits for them, and re-layouts: 13.1 us -> none  [the longest x2 11.7 us: per_device(): blocks.astype(jnp.bfloat16)]
    pallas_call x0 -> x8, Pallas kernels: none -> 11.1 us  [the longest x1 2.89 us: per_device(): pl.pallas_call(up_kernel, grid_spec=pltpu.PrefetchScalarGridSpec(num_scal...]
    ppermute x0 -> x3, starting transfers between devices: none -> 9.3 us  [per_device(): line_weights.append(lax.ppermute(moved, axes, pairs))]
  transfers between devices with their start and end apart: 3 -> 6, of which waited for: 3 -> 3; matrix products, arithmetic and copies ran while one was open for 0% -> 3% of each run, Pallas kernels for 0% -> 1%
where the time goes in v2:
time: 164 us; the launch traced here: 163 us
  waiting for transfers between devices  71.1 us (43%)
  starting transfers between devices  39.1 us (24%)
  blocking collectives  32.8 us (20%)
  Pallas kernels  11.1 us (7%)
  local copies, waits for them, and re-layouts  5.08 us (3%)
  other arithmetic  3.34 us (2%)
    all_to_all x1, waiting for transfers between devices, per_device(): lax.all_to_all(by_source, 'outer', split_axis=0, concat_axis=0, tiled=True)  38.3 us
    all_to_all x3, blocking collectives, exchange(): lax.all_to_all(value, axes, split_axis=0, concat_axis=0, tiled=True, axis...  32.8 us
    all_to_all x1, waiting for transfers between devices, per_device(): lax.all_to_all(packed, 'outer', split_axis=0, concat_axis=0, tiled=True)  24.8 us
    all_to_all x1, starting transfers between devices, per_device(): lax.all_to_all(packed, 'outer', split_axis=0, concat_axis=0, tiled=True)  16.8 us
    ppermute x3, starting transfers between devices, per_device(): line_weights.append(lax.ppermute(moved, axes, pairs))  9.3 us
    all_to_all x1, starting transfers between devices, per_device(): lax.all_to_all(by_source, 'outer', split_axis=0, concat_axis=0, tiled=True)  8.82 us
    all_to_all x1, waiting for transfers between devices, exchange(): lax.all_to_all(value, axes, split_axis=0, concat_axis=0, tiled=True, axis...  7.96 us
    all_to_all x1, starting transfers between devices, exchange(): lax.all_to_all(value, axes, split_axis=0, concat_axis=0, tiled=True, axis...  4.16 us
  transfers between devices with their start and end apart: 6, of which 3 were waited for; matrix products, arithmetic and copies ran while one was open for 3% of the time, Pallas kernels for 1%

profile of v2, /device:TPU:1, one launch (start us, length us, event | category | flops | bytes accessed | tf_op | source)
XLA Modules:
  0.0 162.8 jit_solution(2766716475052584333)
XLA Ops:
  0.0 1.0 copy-done.4
  2.4 0.9 copy-done.2
  3.3 16.8 %all-to-all-start = ((bf16[32,40,256]{2,1,0:T(8,128)(2,1)}), bf16[32,40,256]{2,1,0:T(8,128)(2,1)}, u32[]{:S(2)}, u32[]{:S(2)}) async-start(bf16[32,40,256]{2,1,0:T(8,128)(2,1)} %bitcast.32), calls=%async_computation | async-start | bytes 1310720 | tf_op jit(solution)/shard_map/all_to_all | solution.py:226
  20.2 1.4 dynamic-slice_bitcast_fusion.5
  21.8 1.1 pad_maximum_fusion.2
  22.9 4.4 %collective-permute-start.2 = (bf16[256,2304]{1,0:T(8,128)(2,1)}, bf16[256,2304]{1,0:T(8,128)(2,1)}, u32[]{:S(2)}, u32[]{:S(2)}) collective-permute-start(bf16[256,2304]{1,0:T(8,128)(2,1)} %pad_maximum_fusion.2), channel_id=1, source_target_pairs={{0,12},{4,0},{8,4},{12,8},{1,13},{5,1},{9,5},{13,9},{2,14},{6,2},{... | collective-permute-start | bytes 3538952 | tf_op jit(solution)/shard_map/ppermute | solution.py:216
  27.3 1.1 pad_maximum_fusion.1
  28.4 2.4 %collective-permute-start.1 = (bf16[256,2304]{1,0:T(8,128)(2,1)}, bf16[256,2304]{1,0:T(8,128)(2,1)}, u32[]{:S(2)}, u32[]{:S(2)}) collective-permute-start(bf16[256,2304]{1,0:T(8,128)(2,1)} %pad_maximum_fusion.1), channel_id=1, source_target_pairs={{0,8},{4,12},{8,0},{12,4},{1,9},{5,13},{9,1},{13,5},{2,10},{6,14},... | collective-permute-start | bytes 3538952 | tf_op jit(solution)/shard_map/ppermute | solution.py:216
  30.8 1.1 pad_maximum_fusion
  31.9 2.5 %collective-permute-start = (bf16[256,2304]{1,0:T(8,128)(2,1)}, bf16[256,2304]{1,0:T(8,128)(2,1)}, u32[]{:S(2)}, u32[]{:S(2)}) collective-permute-start(bf16[256,2304]{1,0:T(8,128)(2,1)} %pad_maximum_fusion), channel_id=1, source_target_pairs={{0,4},{4,8},{8,12},{12,0},{1,5},{5,9},{9,13},{13,1},{2,6},{6,10},{... | collective-permute-start | bytes 3538952 | tf_op jit(solution)/shard_map/ppermute | solution.py:216
  34.4 24.8 %all-to-all-done = bf16[32,40,256]{2,1,0:T(8,128)(2,1)} async-done(((bf16[32,40,256]{2,1,0:T(8,128)(2,1)}), bf16[32,40,256]{2,1,0:T(8,128)(2,1)}, u32[]{:S(2)}, u32[]{:S(2)}) %all-to-all-start) | async-done | bytes 655392 | tf_op jit(solution)/shard_map/all_to_all | solution.py:226
  59.2 1.6 to_experts.1
  60.8 0.9 copy-done.3
  61.7 4.2 %all-to-all-start.1 = ((bf16[4,320,256]{2,1,0:T(8,128)(2,1)}), bf16[4,320,256]{2,1,0:T(8,128)(2,1)}, u32[]{:S(2)}, u32[]{:S(2)}) async-start(bf16[4,320,256]{2,1,0:T(8,128)(2,1)} %copy-done.3), calls=%async_computation.1 | async-start | bytes 1310720 | tf_op jit(solution)/shard_map/all_to_all | solution.py:203
  65.9 8.0 %all-to-all-done.1.rows_ref = bf16[4,320,256]{2,1,0:T(8,128)(2,1)} async-done(((bf16[4,320,256]{2,1,0:T(8,128)(2,1)}), bf16[4,320,256]{2,1,0:T(8,128)(2,1)}, u32[]{:S(2)}, u32[]{:S(2)}) %all-to-all-start.1) | async-done | bytes 655392 | tf_op jit(solution)/shard_map/all_to_all | solution.py:203
  73.9 2.9 %gate_up.1 = bf16[4,320,384]{2,1,0:T(8,128)(2,1)S(1)} custom-call(s32[1]{0:T(128)} %bitcast.2.me_ref, bf16[4,320,256]{2,1,0:T(8,128)(2,1)} %all-to-all-done.1.rows_ref, bf16[4,256,1536]{2,1,0:T(8,128)(2,1)S(1)} %copy-done, bf16[256,2304]{1,0:T(8,128)(2,1)} %collective-permute-done.refs_0_, bf16[256,2304]{1,0:T(8,128)(2,1)} %collective-permute-done.1.refs_1_, ...), custom_call_target="tpu_custom_call" | custom-call | flops 1006632960 | bytes 3145728 | tf_op jit(solution)/shard_map/gate_up/pallas_call | solution.py:237
  76.8 13.5 %all_to_all.46.parts_ref = bf16[4,320,384]{2,1,0:T(8,128)(2,1)S(1)} all-to-all(bf16[4,320,384]{2,1,0:T(8,128)(2,1)S(1)} %gate_up.1), channel_id=1, replica_groups={{0,1,2,3},{4,5,6,7},{8,9,10,11},{12,13,14,15},{16,20,24,28},{17,21,25,2..., dimensions={0} | all-to-all | bytes 1966080 | tf_op jit(solution)/shard_map/all_to_all | solution.py:203
  91.2 9.1 %all_to_all.47.hidden_ref = bf16[4,160,384]{2,1,0:T(8,128)(2,1)S(1)} all-to-all(bf16[4,160,384]{2,1,0:T(8,128)(2,1)S(1)} %hidden.1), channel_id=1, replica_groups={{0,1,2,3},{4,5,6,7},{8,9,10,11},{12,13,14,15},{16,20,24,28},{17,21,25,2..., dimensions={0} | all-to-all | bytes 983040 | tf_op jit(solution)/shard_map/all_to_all | solution.py:203
  100.3 1.9 %down.1 = bf16[4,320,256]{2,1,0:T(8,128)(2,1)S(1)} custom-call(s32[1]{0:T(128)} %bitcast.2.me_ref, bf16[4,160,384]{2,1,0:T(8,128)(2,1)S(1)} %all_to_all.47.hidden_ref, bf16[4,768,256]{2,1,0:T(8,128)(2,1)S(1)} %copy-done.1, bf16[256,2304]{1,0:T(8,128)(2,1)} %collective-permute-done.refs_0_, bf16[256,2304]{1,0:T(8,128)(2,1)} %collective-permute-done.1.refs_1_, ...), custom_call_target="tpu_custom_call" | custom-call | flops 503316480 | bytes 1572864 | tf_op jit(solution)/shard_map/down/pallas_call | solution.py:268
  102.3 10.2 %all_to_all.48.rows_ref = bf16[4,320,256]{2,1,0:T(8,128)(2,1)S(1)} all-to-all(bf16[4,320,256]{2,1,0:T(8,128)(2,1)S(1)} %down.1), channel_id=1, replica_groups={{0,4,8,12},{1,5,9,13},{2,6,10,14},{3,7,11,15},{16,17,18,19},{20,21,22,2..., dimensions={0} | all-to-all | bytes 1310720 | tf_op jit(solution)/shard_map/all_to_all | solution.py:203
  112.5 1.4 to_sources.1
  113.8 8.8 %all-to-all-start.5 = ((bf16[32,40,256]{2,1,0:T(8,128)(2,1)}), bf16[32,40,256]{2,1,0:T(8,128)(2,1)S(1)}, u32[]{:S(2)}, u32[]{:S(2)}) async-start(bf16[32,40,256]{2,1,0:T(8,128)(2,1)} %bitcast.17), calls=%async_computation.5 | async-start | bytes 1310720 | tf_op jit(solution)/shard_map/all_to_all | solution.py:300
  123.4 38.3 %all-to-all-done.5 = bf16[32,40,256]{2,1,0:T(8,128)(2,1)S(1)} async-done(((bf16[32,40,256]{2,1,0:T(8,128)(2,1)}), bf16[32,40,256]{2,1,0:T(8,128)(2,1)S(1)}, u32[]{:S(2)}, u32[]{:S(2)}) %all-to-all-start.5) | async-done | bytes 655392 | tf_op jit(solution)/shard_map/all_to_all | solution.py:300
  161.8 1.1 mix.1
  (22 shorter events, 3.2 us)
Async XLA Ops:
  0.0 21.6 %copy-start = (bf16[4,256,1536]{2,1,0:T(8,128)(2,1)S(1)}, bf16[4,256,1536]{2,1,0:T(8,128)(2,1)}, u32[]{:S(2)}) copy-start(bf16[4,256,1536]{2,1,0:T(8,128)(2,1)} %own_ref.2) | copy-start | bytes 9437188
  0.0 1.0 copy-start.4
  1.0 0.7 copy-start.6
  2.4 0.9 copy-start.2
  3.3 56.0 %all-to-all-start = ((bf16[32,40,256]{2,1,0:T(8,128)(2,1)}), bf16[32,40,256]{2,1,0:T(8,128)(2,1)}, u32[]{:S(2)}, u32[]{:S(2)}) async-start(bf16[32,40,256]{2,1,0:T(8,128)(2,1)} %bitcast.32), calls=%async_computation | async-start | bytes 1310720 | tf_op jit(solution)/shard_map/all_to_all | solution.py:226
  22.9 43.0 %collective-permute-start.2 = (bf16[256,2304]{1,0:T(8,128)(2,1)}, bf16[256,2304]{1,0:T(8,128)(2,1)}, u32[]{:S(2)}, u32[]{:S(2)}) collective-permute-start(bf16[256,2304]{1,0:T(8,128)(2,1)} %pad_maximum_fusion.2), channel_id=1, source_target_pairs={{0,12},{4,0},{8,4},{12,8},{1,13},{5,1},{9,5},{13,9},{2,14},{6,2},{... | collective-permute-start | bytes 3538952 | tf_op jit(solution)/shard_map/ppermute | solution.py:216
  28.4 37.5 %collective-permute-start.1 = (bf16[256,2304]{1,0:T(8,128)(2,1)}, bf16[256,2304]{1,0:T(8,128)(2,1)}, u32[]{:S(2)}, u32[]{:S(2)}) collective-permute-start(bf16[256,2304]{1,0:T(8,128)(2,1)} %pad_maximum_fusion.1), channel_id=1, source_target_pairs={{0,8},{4,12},{8,0},{12,4},{1,9},{5,13},{9,1},{13,5},{2,10},{6,14},... | collective-permute-start | bytes 3538952 | tf_op jit(solution)/shard_map/ppermute | solution.py:216
  31.9 34.0 %collective-permute-start = (bf16[256,2304]{1,0:T(8,128)(2,1)}, bf16[256,2304]{1,0:T(8,128)(2,1)}, u32[]{:S(2)}, u32[]{:S(2)}) collective-permute-start(bf16[256,2304]{1,0:T(8,128)(2,1)} %pad_maximum_fusion), channel_id=1, source_target_pairs={{0,4},{4,8},{8,12},{12,0},{1,5},{5,9},{9,13},{13,1},{2,6},{6,10},{... | collective-permute-start | bytes 3538952 | tf_op jit(solution)/shard_map/ppermute | solution.py:216
  60.8 0.9 copy-start.3
  61.7 12.2 %all-to-all-start.1 = ((bf16[4,320,256]{2,1,0:T(8,128)(2,1)}), bf16[4,320,256]{2,1,0:T(8,128)(2,1)}, u32[]{:S(2)}, u32[]{:S(2)}) async-start(bf16[4,320,256]{2,1,0:T(8,128)(2,1)} %copy-done.3), calls=%async_computation.1 | async-start | bytes 1310720 | tf_op jit(solution)/shard_map/all_to_all | solution.py:203
  76.8 23.5 %copy-start.1 = (bf16[4,768,256]{2,1,0:T(8,128)(2,1)S(1)}, bf16[4,768,256]{2,1,0:T(8,128)(2,1)}, u32[]{:S(2)}) copy-start(bf16[4,768,256]{2,1,0:T(8,128)(2,1)} %own_ref.3) | copy-start | bytes 4718596
  102.3 20.4 %copy-start.7 = (s32[128,8]{0,1:T(8,128)S(1)}, s32[128,8]{0,1:T(8,128)}, u32[]{:S(2)}) copy-start(s32[128,8]{0,1:T(8,128)} %param.6) | copy-start | bytes 12292
  102.3 20.4 %copy-start.8 = (f32[128,8]{0,1:T(8,128)S(1)}, f32[128,8]{0,1:T(8,128)}, u32[]{:S(2)}) copy-start(f32[128,8]{0,1:T(8,128)} %param.7) | copy-start | bytes 12292
  102.3 59.5 %copy-start.5 = (bf16[128,256]{1,0:T(8,128)(2,1)S(1)}, bf16[128,256]{1,0:T(8,128)(2,1)}, u32[]{:S(2)}) copy-start(bf16[128,256]{1,0:T(8,128)(2,1)} %tokens_ref.3) | copy-start | bytes 196612
  113.8 47.9 %all-to-all-start.5 = ((bf16[32,40,256]{2,1,0:T(8,128)(2,1)}), bf16[32,40,256]{2,1,0:T(8,128)(2,1)S(1)}, u32[]{:S(2)}, u32[]{:S(2)}) async-start(bf16[32,40,256]{2,1,0:T(8,128)(2,1)} %bitcast.17), calls=%async_computation.5 | async-start | bytes 1310720 | tf_op jit(solution)/shard_map/all_to_all | solution.py:300

commit v3 on v2

v3 whole, which is shorter than its diff:
```python
import functools

import jax
import jax.numpy as jnp
from jax import lax
from jax.experimental import pallas as pl
from jax.experimental.pallas import tpu as pltpu
from jax.sharding import PartitionSpec as P

F32 = jnp.float32
BF16 = jnp.bfloat16
VMEM_LIMIT = 40 * 1024 * 1024


def iota(shape, dim):
    return lax.broadcasted_iota(jnp.int32, shape, dim)


def dot(a, b, contract=((1,), (0,))):
    return lax.dot_general(a, b, (contract, ((), ())), preferred_element_type=F32)


def slot_codes(named):
    rows = named.shape[1]
    earlier = jnp.where(iota((rows, rows), 0) < iota((rows, rows), 1), 1.0, 0.0).astype(BF16)
    rank = dot(named.astype(BF16), earlier)
    return named * (rank + 1.0)


def message_rows(group, shape, dim, fold):
    row = iota(shape, dim)
    each = shape[dim] // group
    position = row // each
    rest = row % each
    return (rest // 2) * group + position, (rest % 2) * fold + 1


def routed(routes_ref, experts):
    top, rows = routes_ref.shape
    expert = iota((experts, rows), 0)
    named = jnp.zeros((experts, rows), F32)
    for k in range(top):
        named = named + jnp.where(routes_ref[k : k + 1, :] == expert, 1.0, 0.0)
    return named


def pack_kernel(group, experts, fold, routes_ref, tokens_ref, packed_ref):
    count = packed_ref.shape[0]
    features = tokens_ref.shape[1]
    code = slot_codes(routed(routes_ref, experts)).astype(BF16)
    expert, first = message_rows(group, (count, 1), 0, fold)
    spread = jnp.where(expert == iota((count, experts), 1), 1.0, 0.0).astype(BF16)
    seen = dot(spread, code) - first.astype(F32)
    tokens = tokens_ref[...]
    for q in range(fold):
        placing = jnp.where(seen == q, 1.0, 0.0).astype(BF16)
        packed_ref[:, q * features : (q + 1) * features] = dot(placing, tokens).astype(BF16)


def gate_kernel(group, experts, fold, routes_ref, gates_ref, weights_ref):
    top, rows = routes_ref.shape
    count = weights_ref.shape[2] // fold
    expert = iota((experts, rows), 0)
    gate = jnp.zeros((experts, rows), F32)
    for k in range(top):
        gate = gate + jnp.where(routes_ref[k : k + 1, :] == expert, gates_ref[k : k + 1, :], 0.0)
    code = slot_codes(routed(routes_ref, experts)).T.astype(BF16)
    gate = gate.T
    expert, first = message_rows(group, (1, count), 1, fold)
    spread = jnp.where(expert == iota((experts, count), 0), 1.0, 0.0).astype(BF16)
    seen = dot(code, spread) - first.astype(F32)
    for part in range(weights_ref.shape[0]):
        piece = gate.astype(BF16)
        gate = gate - piece.astype(F32)
        chosen = dot(piece, spread)
        for q in range(fold):
            weights_ref[part, :, q * count : (q + 1) * count] = jnp.where(
                seen == q, chosen, 0.0
            ).astype(BF16)


def up_kernel(fold, me_ref, arrived_ref, own_ref, *refs):
    others, out_ref, rows_ref = refs[:-2], refs[-2], refs[-1]
    side, _, features = rows_ref.shape
    each = arrived_ref.shape[0] // side
    tile = out_ref.shape[2]

    @pl.when(pl.program_id(0) == 0)
    def _():
        for s in range(side):
            for q in range(fold):
                rows_ref[s, q * each : (q + 1) * each, :] = arrived_ref[
                    s * each : (s + 1) * each, q * features : (q + 1) * features
                ]

    total = dot(rows_ref[me_ref[0]], own_ref[0])
    for k, w_ref in enumerate(others, 1):
        total = total + dot(rows_ref[lax.rem(me_ref[0] + side - k, side)], w_ref[...])
    for n in range(out_ref.shape[0]):
        out_ref[n] = total[:, n * tile : (n + 1) * tile].astype(BF16)


def hidden_kernel(share, parts_ref, out_ref):
    total = parts_ref[0].astype(F32)
    for n in range(1, parts_ref.shape[0]):
        total = total + parts_ref[n].astype(F32)
    width = total.shape[1]
    up = pltpu.roll(total, width - share, 1)
    mixed = (total / (1.0 + jnp.exp(-total)) * up).astype(BF16)
    column = iota((width, 1), 0)
    block = jnp.zeros_like(column)
    for n in range(1, width // (2 * share)):
        block = block + jnp.where(column >= 2 * share * n, 1, 0)
    unit = jnp.where(column - 2 * share * block < share, column - share * block, -width)
    lane = iota((width, width), 1)
    left = jnp.where(unit == lane, 1.0, 0.0).astype(BF16)
    right = jnp.where(unit + width // 2 == lane, 1.0, 0.0).astype(BF16)
    half = total.shape[0] // 2
    hidden = (dot(mixed[:half], left) + dot(mixed[half:], right)).astype(BF16)
    for n in range(out_ref.shape[0]):
        out_ref[n] = hidden


def down_kernel(batches, fold, me_ref, hidden_ref, own_ref, *refs):
    others, out_ref = refs[:-1], refs[-1]
    side, packed, width = hidden_ref.shape
    each = out_ref.shape[0] // side
    features = out_ref.shape[1] // fold
    half = packed // batches
    left = jnp.concatenate([hidden_ref[b, :, : width // 2] for b in range(side)], axis=1)
    right = jnp.concatenate([hidden_ref[b, :, width // 2 :] for b in range(side)], axis=1)
    pieces = []
    for n in range(batches):
        pieces += [left[n * half : (n + 1) * half], right[n * half : (n + 1) * half]]
    hidden = jnp.concatenate(pieces, axis=0)
    for k in range(side):
        w = own_ref[0] if k == 0 else others[k - 1][...]
        made = dot(hidden, w).astype(BF16)
        place = lax.rem(me_ref[0] + side - k, side) if k else me_ref[0]
        for q in range(fold):
            out_ref[
                pl.ds(pl.multiple_of(place * each, each), each), q * features : (q + 1) * features
            ] = made[q * each : (q + 1) * each]


def keep_kernel(*refs):
    sem = refs[-1]
    parts, outs = refs[: len(refs) // 2], refs[len(refs) // 2 : -1]
    copies = [pltpu.make_async_copy(p, o, sem.at[n]) for n, (p, o) in enumerate(zip(parts, outs))]
    for copy in copies:
        copy.start()
    for copy in copies:
        copy.wait()


def mix_kernel(fold, tokens_ref, weights_ref, home_ref, out_ref):
    features = tokens_ref.shape[1]
    home = jnp.concatenate(
        [home_ref[:, q * features : (q + 1) * features] for q in range(fold)], axis=0
    )
    total = tokens_ref[...].astype(F32)
    for part in range(weights_ref.shape[0]):
        total = total + dot(weights_ref[part], home)
    out_ref[...] = total.astype(BF16)


def params(*semantics):
    return pltpu.CompilerParams(
        dimension_semantics=semantics or None, vmem_limit_bytes=VMEM_LIMIT
    )


def cost(flops, nbytes):
    return pl.CostEstimate(flops=flops, bytes_accessed=nbytes, transcendentals=0)


def per_device(mesh_shape, tokens, routes, gates, w_gate_up, w_down):
    rows, features = tokens.shape
    outer, inner = mesh_shape
    group, _, columns = w_gate_up.shape
    hidden = w_down.shape[1]
    experts = group * outer
    cap = 10
    slots = experts * cap
    per_expert = outer * cap
    side = group
    fold = cap // 2
    count = 2 * experts
    across = [[y * side + x for x in range(side)] for y in range(side)]
    along = [[y * side + x for y in range(side)] for x in range(side)]
    column = [[o * inner + n for n in line for o in range(outer)] for line in along]
    me = lax.axis_index("inner") // side
    me_ref = me.astype(jnp.int32).reshape(1)
    in_hbm = functools.partial(pltpu.with_memory_space_constraint, memory_space=pltpu.HBM)

    def exchange(value, axes, groups):
        return lax.all_to_all(
            value, axes, split_axis=0, concat_axis=0, tiled=True, axis_index_groups=groups
        )

    def to_column(messages):
        messages = messages.reshape(experts, 2, fold * features)
        return exchange(messages, ("outer", "inner"), column).reshape(count, fold * features)

    def from_line(weights, k):
        pairs = [(line[n], line[(n + k) % side]) for line in along for n in range(side)]
        share = lax.dynamic_index_in_dim(weights, (me + k) % side, 0, keepdims=False)
        return lax.ppermute(share, "inner", pairs)

    def keep(parts, weight, name):
        return pl.pallas_call(
            keep_kernel,
            in_specs=[pl.BlockSpec(memory_space=pltpu.VMEM)] * len(parts),
            out_specs=[pl.BlockSpec(memory_space=pltpu.HBM)] * len(parts),
            out_shape=[pltpu.HBM(part.shape, BF16) for part in parts],
            scratch_shapes=[pltpu.SemaphoreType.DMA((len(parts),))],
            compiler_params=params(),
            cost_estimate=cost(weight, 4 * len(parts) * parts[0].size),
            name=name,
        )(*parts)

    up_weights = [from_line(w_gate_up, k) for k in range(1, side)]
    up_weights[1:2] = keep(up_weights[1:2], 20000000000, "keep_up")
    up_weights = [in_hbm(part) for part in up_weights]
    down_weights = keep([from_line(w_down, k) for k in range(1, side)], 20000000000, "keep_down")
    routes, gates = routes.T, gates.T

    packed = pl.pallas_call(
        functools.partial(pack_kernel, group, experts, fold),
        out_shape=jax.ShapeDtypeStruct((count, fold * features), BF16),
        compiler_params=params(),
        cost_estimate=cost(4 * slots * rows * features, 2 * slots * features),
        name="pack",
    )(routes, tokens)
    arrived = to_column(packed)

    tile = columns // side
    partial_value = pl.pallas_call(
        functools.partial(up_kernel, fold),
        grid_spec=pltpu.PrefetchScalarGridSpec(
            num_scalar_prefetch=1,
            grid=(side // 2,),
            in_specs=[
                pl.BlockSpec((count, fold * features), lambda c, me: (0, 0)),
                pl.BlockSpec((1, features, 2 * tile), lambda c, me: (me[0], 0, c)),
            ]
            + [pl.BlockSpec((features, 2 * tile), lambda c, me: (0, c))] * (side - 1),
            out_specs=pl.BlockSpec((2, per_expert, tile), lambda c, me: (c, 0, 0)),
            scratch_shapes=[pltpu.VMEM((side, per_expert, features), BF16)],
        ),
        out_shape=jax.ShapeDtypeStruct((side, per_expert, tile), BF16),
        compiler_params=params("arbitrary"),
        cost_estimate=cost(2 * slots * features * columns, 8 * features * columns),
        name="gate_up",
    )(me_ref, arrived, in_hbm(w_gate_up), *up_weights)
    swapped = exchange(partial_value.reshape(side * per_expert, tile), "inner", across)
    swapped, *down_weights = lax.optimization_barrier((swapped, *down_weights))
    batches = 2
    packed_rows = per_expert // 2
    mine = pl.pallas_call(
        functools.partial(hidden_kernel, hidden // inner),
        grid=(batches,),
        in_specs=[pl.BlockSpec((side, per_expert // batches, tile), lambda n: (0, n, 0))],
        out_specs=pl.BlockSpec((side, packed_rows // batches, tile), lambda n: (0, n, 0)),
        out_shape=jax.ShapeDtypeStruct((side, packed_rows, tile), BF16),
        compiler_params=params("arbitrary"),
        cost_estimate=cost(per_expert * tile * tile, 4 * per_expert * tile * side),
        name="hidden",
    )(swapped.reshape(side, per_expert, tile))
    gathered = exchange(mine.reshape(side * packed_rows, tile), "inner", across)
    expert_out = pl.pallas_call(
        functools.partial(down_kernel, batches, fold),
        grid_spec=pltpu.PrefetchScalarGridSpec(
            num_scalar_prefetch=1,
            grid=(1,),
            in_specs=[
                pl.BlockSpec((side, packed_rows, tile), lambda n, me: (0, 0, 0)),
                pl.BlockSpec((1, hidden, features), lambda n, me: (me[0], 0, 0)),
            ]
            + [pl.BlockSpec((hidden, features), lambda n, me: (0, 0))] * (side - 1),
            out_specs=pl.BlockSpec((count, fold * features), lambda n, me: (0, 0)),
        ),
        out_shape=jax.ShapeDtypeStruct((count, fold * features), BF16),
        compiler_params=params("arbitrary"),
        cost_estimate=cost(2 * slots * features * hidden, 8 * features * hidden),
        name="down",
    )(me_ref, gathered.reshape(side, packed_rows, tile), in_hbm(w_down), *map(in_hbm, down_weights))
    weights = pl.pallas_call(
        functools.partial(gate_kernel, group, experts, fold),
        out_shape=jax.ShapeDtypeStruct((3, rows, slots), BF16),
        compiler_params=params(),
        cost_estimate=cost(2 * rows * experts * slots, 6 * rows * slots),
        name="gate_weights",
    )(routes, gates)
    home = to_column(expert_out)
    return pl.pallas_call(
        functools.partial(mix_kernel, fold),
        out_shape=jax.ShapeDtypeStruct((rows, features), BF16),
        compiler_params=params(),
        cost_estimate=cost(6 * rows * slots * features, 2 * slots * features),
        name="mix",
    )(tokens, weights, home)


def solution(mesh):
    in_specs = (
        P("outer", "inner"),
        P("outer", None),
        P("outer", None),
        P("outer", "inner", None),
        P("outer", None, "inner"),
    )
    return jax.shard_map(
        functools.partial(per_device, (mesh.shape["outer"], mesh.shape["inner"])),
        mesh=mesh,
        in_specs=in_specs,
        out_specs=P("outer", "inner"),
        check_vma=False,
    )
```

time: 164 us -> 158 us (0.963)
  blocking collectives: 32.8 us -> 9.15 us
  starting transfers between devices: 39.1 us -> 58.1 us
  local copies, waits for them, and re-layouts: 5.08 us -> 9.71 us
  other arithmetic: 3.34 us -> 0 us
  waiting for transfers between devices: 71.1 us -> 69 us
    all_to_all x2 -> x0, waiting for transfers between devices: 63.1 us -> none  [the longest x1 38.3 us: per_device(): lax.all_to_all(by_source, 'outer', split_axis=0, concat_axis=0, tiled=True)]
    all_to_all x1 -> x3, waiting for transfers between devices: 7.96 us -> 69 us  [exchange(): lax.all_to_all(value, axes, split_axis=0, concat_axis=0, tiled=True, axis...]
    all_to_all x1 -> x3, starting transfers between devices: 4.16 us -> 36.2 us  [exchange(): lax.all_to_all(value, axes, split_axis=0, concat_axis=0, tiled=True, axis...]
    all_to_all x2 -> x0, starting transfers between devices: 25.6 us -> none  [the longest x1 16.8 us: per_device(): lax.all_to_all(packed, 'outer', split_axis=0, concat_axis=0, tiled=True)]
    all_to_all x3 -> x1, blocking collectives: 32.8 us -> 9.15 us  [exchange(): lax.all_to_all(value, axes, split_axis=0, concat_axis=0, tiled=True, axis...]
    ppermute x3 -> x6, starting transfers between devices: 9.3 us -> 21.9 us  [from_line(): return lax.ppermute(share, 'inner', pairs)]
    reshape x0 -> x4, local copies, waits for them, and re-layouts: none -> 4.51 us  [the longest x2 2.32 us: to_column(): exchange(messages, ('outer', 'inner'), column)]
    squeeze x1 -> x2, local copies, waits for them, and re-layouts: 0.16 us -> 4.3 us  [from_line(): lax.dynamic_index_in_dim(weights, (me + k) % side, 0, keepdims=False)]
  transfers between devices with their start and end apart: 6 -> 9, of which waited for: 3 -> 3; matrix products, arithmetic and copies ran while one was open for 3% -> 3% of each run, Pallas kernels for 1% -> 4%
where the time goes in v3:
time: 158 us; the launch traced here: 157 us
  waiting for transfers between devices  69 us (44%)
  starting transfers between devices  58.1 us (37%)
  Pallas kernels  10.7 us (7%)
  local copies, waits for them, and re-layouts  9.71 us (6%)
  blocking collectives  9.15 us (6%)
    all_to_all x3, waiting for transfers between devices, exchange(): lax.all_to_all(value, axes, split_axis=0, concat_axis=0, tiled=True, axis...  69 us
    all_to_all x3, starting transfers between devices, exchange(): lax.all_to_all(value, axes, split_axis=0, concat_axis=0, tiled=True, axis...  36.2 us
    ppermute x6, starting transfers between devices, from_line(): return lax.ppermute(share, 'inner', pairs)  21.9 us
    all_to_all x1, blocking collectives, exchange(): lax.all_to_all(value, axes, split_axis=0, concat_axis=0, tiled=True, axis...  9.15 us
    squeeze x2, local copies, waits for them, and re-layouts, from_line(): lax.dynamic_index_in_dim(weights, (me + k) % side, 0, keepdims=False)  4.3 us
    pallas_call x1, Pallas kernels, per_device(): pl.pallas_call(functools.partial(up_kernel, fold), grid_spec=pltpu.Prefet...  3.61 us
  transfers between devices with their start and end apart: 9, of which 3 were waited for; matrix products, arithmetic and copies ran while one was open for 3% of the time, Pallas kernels for 4%

profile of v3, /device:TPU:1, one launch (start us, length us, event | category | flops | bytes accessed | tf_op | source)
XLA Modules:
  0.0 156.9 jit_solution(6700395323414618011)
XLA Ops:
  0.0 3.2 %dynamic-slice_bitcast_fusion = (bf16[256,1536]{1,0:T(8,128)(2,1)}, bf16[256,1536]{1,0:T(8,128)(2,1)}, bf16[256,1536]{1,0:T(8,128)(2,1)}) fusion(bf16[4,256,1536]{2,1,0:T(8,128)(2,1)} %own_ref.2, s32[]{:T(128)S(6)} %select_n.45, s32[]{:T(128)S(6)} %select_n.43, s32[]{:T(128)S(6)} %select_n.41), kind=kLoop, calls=%fused_computation | loop fusion | bytes 4718604 | tf_op jit(solution)/shard_map/jit(dynamic_index_in_dim)/squeeze | solution.py:207
  3.2 5.6 %collective-permute-start.1 = (bf16[256,1536]{1,0:T(8,128)(2,1)}, bf16[256,1536]{1,0:T(8,128)(2,1)S(1)}, u32[]{:S(2)}, u32[]{:S(2)}) collective-permute-start(bf16[256,1536]{1,0:T(8,128)(2,1)} %get-tuple-element.20), channel_id=1, source_target_pairs={{0,8},{4,12},{8,0},{12,4},{1,9},{5,13},{9,1},{13,5},{2,10},{6,14},... | collective-permute-start | bytes 2359304 | tf_op jit(solution)/shard_map/ppermute | solution.py:208
  9.5 1.1 reshape.29
  10.6 18.3 %all-to-all-start = ((bf16[128,2,1280]{2,1,0:T(2,128)(2,1)}), bf16[128,2,1280]{2,1,0:T(2,128)(2,1)}, u32[]{:S(2)}, u32[]{:S(2)}) async-start(bf16[128,2,1280]{2,1,0:T(2,128)(2,1)} %reshape.29), calls=%async_computation | async-start | bytes 1310720 | tf_op jit(solution)/shard_map/all_to_all | solution.py:197
  28.9 3.4 %collective-permute-start = (bf16[256,1536]{1,0:T(8,128)(2,1)}, bf16[256,1536]{1,0:T(8,128)(2,1)S(1)}, u32[]{:S(2)}, u32[]{:S(2)}) collective-permute-start(bf16[256,1536]{1,0:T(8,128)(2,1)} %get-tuple-element.21), channel_id=1, source_target_pairs={{0,4},{4,8},{8,12},{12,0},{1,5},{5,9},{9,13},{13,1},{2,6},{6,10},{... | collective-permute-start | bytes 2359304 | tf_op jit(solution)/shard_map/ppermute | solution.py:208
  32.3 3.6 %collective-permute-start.2 = (bf16[256,1536]{1,0:T(8,128)(2,1)}, bf16[256,1536]{1,0:T(8,128)(2,1)}, u32[]{:S(2)}, u32[]{:S(2)}) collective-permute-start(bf16[256,1536]{1,0:T(8,128)(2,1)} %get-tuple-element.19), channel_id=1, source_target_pairs={{0,12},{4,0},{8,4},{12,8},{1,13},{5,1},{9,5},{13,9},{2,14},{6,2},{... | collective-permute-start | bytes 2359304 | tf_op jit(solution)/shard_map/ppermute | solution.py:208
  35.9 1.1 dynamic-slice_bitcast_fusion.3
  37.0 1.9 %collective-permute-start.3 = (bf16[768,256]{1,0:T(8,128)(2,1)}, bf16[768,256]{1,0:T(8,128)(2,1)S(1)}, u32[]{:S(2)}, u32[]{:S(2)}) collective-permute-start(bf16[768,256]{1,0:T(8,128)(2,1)} %get-tuple-element.24), channel_id=1, source_target_pairs={{0,4},{4,8},{8,12},{12,0},{1,5},{5,9},{9,13},{13,1},{2,6},{6,10},{... | collective-permute-start | bytes 1179656 | tf_op jit(solution)/shard_map/ppermute | solution.py:208
  38.9 4.5 %collective-permute-start.4 = (bf16[768,256]{1,0:T(8,128)(2,1)}, bf16[768,256]{1,0:T(8,128)(2,1)S(1)}, u32[]{:S(2)}, u32[]{:S(2)}) collective-permute-start(bf16[768,256]{1,0:T(8,128)(2,1)} %get-tuple-element.23), channel_id=1, source_target_pairs={{0,8},{4,12},{8,0},{12,4},{1,9},{5,13},{9,1},{13,5},{2,10},{6,14},... | collective-permute-start | bytes 1179656 | tf_op jit(solution)/shard_map/ppermute | solution.py:208
  43.4 2.9 %collective-permute-start.5 = (bf16[768,256]{1,0:T(8,128)(2,1)}, bf16[768,256]{1,0:T(8,128)(2,1)S(1)}, u32[]{:S(2)}, u32[]{:S(2)}) collective-permute-start(bf16[768,256]{1,0:T(8,128)(2,1)} %get-tuple-element.22), channel_id=1, source_target_pairs={{0,12},{4,0},{8,4},{12,8},{1,13},{5,1},{9,5},{13,9},{2,14},{6,2},{... | collective-permute-start | bytes 1179656 | tf_op jit(solution)/shard_map/ppermute | solution.py:208
  46.3 0.9 keep_up.1.refs_1_
  47.2 19.7 %all-to-all-done = bf16[128,2,1280]{2,1,0:T(2,128)(2,1)} async-done(((bf16[128,2,1280]{2,1,0:T(2,128)(2,1)}), bf16[128,2,1280]{2,1,0:T(2,128)(2,1)}, u32[]{:S(2)}, u32[]{:S(2)}) %all-to-all-start) | async-done | bytes 655392 | tf_op jit(solution)/shard_map/all_to_all | solution.py:197
  66.9 2.1 %reshape.30.arrived_ref = bf16[256,1280]{1,0:T(8,128)(2,1)S(1)} reshape(bf16[128,2,1280]{2,1,0:T(2,128)(2,1)} %all-to-all-done) | data formatting | bytes 1310720 | tf_op jit(solution)/shard_map/reshape | solution.py:203
  69.0 0.9 copy-done.4
  69.9 3.6 %gate_up.1 = bf16[4,320,384]{2,1,0:T(8,128)(2,1)} custom-call(s32[1]{0:T(128)} %bitcast.2.me_ref, bf16[256,1280]{1,0:T(8,128)(2,1)S(1)} %reshape.30.arrived_ref, bf16[4,256,1536]{2,1,0:T(8,128)(2,1)} %own_ref.2, bf16[256,1536]{1,0:T(8,128)(2,1)} %copy-done.4, bf16[256,1536]{1,0:T(8,128)(2,1)} %keep_up.1.refs_1_, bf16[256,1536]{1,0:T(8,128)(2,1)} %collective-permute-done.2.refs_2_), custom_call_target="tpu_custom_call" | custom-call | flops 1006632960 | bytes 3145728 | tf_op jit(solution)/shard_map/gate_up/pallas_call | solution.py:238
  73.5 4.0 %all-to-all-start.1 = ((bf16[4,320,384]{2,1,0:T(8,128)(2,1)}), bf16[4,320,384]{2,1,0:T(8,128)(2,1)S(1)}, u32[]{:S(2)}, u32[]{:S(2)}) async-start(bf16[4,320,384]{2,1,0:T(8,128)(2,1)} %gate_up.1), calls=%async_computation.1 | async-start | bytes 1966080 | tf_op jit(solution)/shard_map/all_to_all | solution.py:197
  77.5 1.1 keep_down.1
  78.6 11.6 %all-to-all-done.1 = bf16[4,320,384]{2,1,0:T(8,128)(2,1)S(1)} async-done(((bf16[4,320,384]{2,1,0:T(8,128)(2,1)}), bf16[4,320,384]{2,1,0:T(8,128)(2,1)S(1)}, u32[]{:S(2)}, u32[]{:S(2)}) %all-to-all-start.1) | async-done | bytes 983072 | tf_op jit(solution)/shard_map/all_to_all | solution.py:197
  91.1 9.1 %all_to_all.25.hidden_ref = bf16[4,160,384]{2,1,0:T(8,128)(2,1)S(1)} all-to-all(bf16[4,160,384]{2,1,0:T(8,128)(2,1)S(1)} %hidden.1), channel_id=1, replica_groups={{0,1,2,3},{4,5,6,7},{8,9,10,11},{12,13,14,15},{16,17,18,19},{20,21,22,2..., dimensions={0} | all-to-all | bytes 983040 | tf_op jit(solution)/shard_map/all_to_all | solution.py:197
  100.2 2.1 %down.1 = bf16[256,1280]{1,0:T(8,128)(2,1)S(1)} custom-call(s32[1]{0:T(128)} %bitcast.2.me_ref, bf16[4,160,384]{2,1,0:T(8,128)(2,1)S(1)} %all_to_all.25.hidden_ref, bf16[4,768,256]{2,1,0:T(8,128)(2,1)} %own_ref.3, bf16[768,256]{1,0:T(8,128)(2,1)} %get-tuple-element.16.refs_0_, bf16[768,256]{1,0:T(8,128)(2,1)} %get-tuple-element.17.refs_1_, ...), custom_call_target="tpu_custom_call" | custom-call | flops 503316480 | bytes 1572864 | tf_op jit(solution)/shard_map/down/pallas_call | solution.py:271
  102.3 1.1 reshape.32
  103.4 13.9 %all-to-all-start.3 = ((bf16[128,2,1280]{2,1,0:T(2,128)(2,1)}), bf16[128,2,1280]{2,1,0:T(2,128)(2,1)S(1)}, u32[]{:S(2)}, u32[]{:S(2)}) async-start(bf16[128,2,1280]{2,1,0:T(2,128)(2,1)} %reshape.32), calls=%async_computation.3 | async-start | bytes 1310720 | tf_op jit(solution)/shard_map/all_to_all | solution.py:197
  117.9 37.7 %all-to-all-done.3 = bf16[128,2,1280]{2,1,0:T(2,128)(2,1)S(1)} async-done(((bf16[128,2,1280]{2,1,0:T(2,128)(2,1)}), bf16[128,2,1280]{2,1,0:T(2,128)(2,1)S(1)}, u32[]{:S(2)}, u32[]{:S(2)}) %all-to-all-start.3) | async-done | bytes 655392 | tf_op jit(solution)/shard_map/all_to_all | solution.py:197
  155.9 1.1 mix.1
  (19 shorter events, 2.3 us)
Async XLA Ops:
  0.0 8.9 %copy-start = (bf16[128,256]{1,0:T(8,128)(2,1)S(1)}, bf16[128,256]{1,0:T(8,128)(2,1)}, u32[]{:S(2)}) copy-start(bf16[128,256]{1,0:T(8,128)(2,1)} %tokens_ref.3) | copy-start | bytes 196612
  0.0 8.9 %copy-start.1 = (s32[128,8]{0,1:T(8,128)S(1)}, s32[128,8]{0,1:T(8,128)}, u32[]{:S(2)}) copy-start(s32[128,8]{0,1:T(8,128)} %param.6) | copy-start | bytes 12292
  0.0 35.9 %copy-start.3 = (bf16[4,768,256]{2,1,0:T(8,128)(2,1)S(1)}, bf16[4,768,256]{2,1,0:T(8,128)(2,1)}, u32[]{:S(2)}) copy-start(bf16[4,768,256]{2,1,0:T(8,128)(2,1)} %own_ref.3) | copy-start | bytes 4718596
  3.2 40.2 %collective-permute-start.1 = (bf16[256,1536]{1,0:T(8,128)(2,1)}, bf16[256,1536]{1,0:T(8,128)(2,1)S(1)}, u32[]{:S(2)}, u32[]{:S(2)}) collective-permute-start(bf16[256,1536]{1,0:T(8,128)(2,1)} %get-tuple-element.20), channel_id=1, source_target_pairs={{0,8},{4,12},{8,0},{12,4},{1,9},{5,13},{9,1},{13,5},{2,10},{6,14},... | collective-permute-start | bytes 2359304 | tf_op jit(solution)/shard_map/ppermute | solution.py:208
  10.6 56.3 %all-to-all-start = ((bf16[128,2,1280]{2,1,0:T(2,128)(2,1)}), bf16[128,2,1280]{2,1,0:T(2,128)(2,1)}, u32[]{:S(2)}, u32[]{:S(2)}) async-start(bf16[128,2,1280]{2,1,0:T(2,128)(2,1)} %reshape.29), calls=%async_computation | async-start | bytes 1310720 | tf_op jit(solution)/shard_map/all_to_all | solution.py:197
  28.9 40.1 %collective-permute-start = (bf16[256,1536]{1,0:T(8,128)(2,1)}, bf16[256,1536]{1,0:T(8,128)(2,1)S(1)}, u32[]{:S(2)}, u32[]{:S(2)}) collective-permute-start(bf16[256,1536]{1,0:T(8,128)(2,1)} %get-tuple-element.21), channel_id=1, source_target_pairs={{0,4},{4,8},{8,12},{12,0},{1,5},{5,9},{9,13},{13,1},{2,6},{6,10},{... | collective-permute-start | bytes 2359304 | tf_op jit(solution)/shard_map/ppermute | solution.py:208
  32.3 36.7 %collective-permute-start.2 = (bf16[256,1536]{1,0:T(8,128)(2,1)}, bf16[256,1536]{1,0:T(8,128)(2,1)}, u32[]{:S(2)}, u32[]{:S(2)}) collective-permute-start(bf16[256,1536]{1,0:T(8,128)(2,1)} %get-tuple-element.19), channel_id=1, source_target_pairs={{0,12},{4,0},{8,4},{12,8},{1,13},{5,1},{9,5},{13,9},{2,14},{6,2},{... | collective-permute-start | bytes 2359304 | tf_op jit(solution)/shard_map/ppermute | solution.py:208
  37.0 40.5 %collective-permute-start.3 = (bf16[768,256]{1,0:T(8,128)(2,1)}, bf16[768,256]{1,0:T(8,128)(2,1)S(1)}, u32[]{:S(2)}, u32[]{:S(2)}) collective-permute-start(bf16[768,256]{1,0:T(8,128)(2,1)} %get-tuple-element.24), channel_id=1, source_target_pairs={{0,4},{4,8},{8,12},{12,0},{1,5},{5,9},{9,13},{13,1},{2,6},{6,10},{... | collective-permute-start | bytes 1179656 | tf_op jit(solution)/shard_map/ppermute | solution.py:208
  38.9 38.6 %collective-permute-start.4 = (bf16[768,256]{1,0:T(8,128)(2,1)}, bf16[768,256]{1,0:T(8,128)(2,1)S(1)}, u32[]{:S(2)}, u32[]{:S(2)}) collective-permute-start(bf16[768,256]{1,0:T(8,128)(2,1)} %get-tuple-element.23), channel_id=1, source_target_pairs={{0,8},{4,12},{8,0},{12,4},{1,9},{5,13},{9,1},{13,5},{2,10},{6,14},... | collective-permute-start | bytes 1179656 | tf_op jit(solution)/shard_map/ppermute | solution.py:208
  43.4 34.1 %collective-permute-start.5 = (bf16[768,256]{1,0:T(8,128)(2,1)}, bf16[768,256]{1,0:T(8,128)(2,1)S(1)}, u32[]{:S(2)}, u32[]{:S(2)}) collective-permute-start(bf16[768,256]{1,0:T(8,128)(2,1)} %get-tuple-element.22), channel_id=1, source_target_pairs={{0,12},{4,0},{8,4},{12,8},{1,13},{5,1},{9,5},{13,9},{2,14},{6,2},{... | collective-permute-start | bytes 1179656 | tf_op jit(solution)/shard_map/ppermute | solution.py:208
  69.0 0.9 copy-start.4
  73.5 16.7 %all-to-all-start.1 = ((bf16[4,320,384]{2,1,0:T(8,128)(2,1)}), bf16[4,320,384]{2,1,0:T(8,128)(2,1)S(1)}, u32[]{:S(2)}, u32[]{:S(2)}) async-start(bf16[4,320,384]{2,1,0:T(8,128)(2,1)} %gate_up.1), calls=%async_computation.1 | async-start | bytes 1966080 | tf_op jit(solution)/shard_map/all_to_all | solution.py:197
  100.2 17.1 %copy-start.2 = (f32[128,8]{0,1:T(8,128)S(1)}, f32[128,8]{0,1:T(8,128)}, u32[]{:S(2)}) copy-start(f32[128,8]{0,1:T(8,128)} %param.7) | copy-start | bytes 12292
  103.4 52.2 %all-to-all-start.3 = ((bf16[128,2,1280]{2,1,0:T(2,128)(2,1)}), bf16[128,2,1280]{2,1,0:T(2,128)(2,1)S(1)}, u32[]{:S(2)}, u32[]{:S(2)}) async-start(bf16[128,2,1280]{2,1,0:T(2,128)(2,1)} %reshape.32), calls=%async_computation.3 | async-start | bytes 1310720 | tf_op jit(solution)/shard_map/all_to_all | solution.py:197

commit v4 on v3

--- a/solution.py
+++ b/solution.py
@@ -44,7 +44,15 @@
     return named
 
 
-def pack_kernel(group, experts, fold, routes_ref, tokens_ref, packed_ref):
+def pack_kernel(group, experts, fold, routes_in, tokens_in, packed_ref, routes_ref, tokens_ref, sem):
+    loads = [
+        pltpu.make_async_copy(routes_in, routes_ref, sem.at[0]),
+        pltpu.make_async_copy(tokens_in, tokens_ref, sem.at[1]),
+    ]
+    for load in loads:
+        load.start()
+    for load in loads:
+        load.wait()
     count = packed_ref.shape[0]
     features = tokens_ref.shape[1]
     code = slot_codes(routed(routes_ref, experts)).astype(BF16)
@@ -143,6 +151,14 @@
             ] = made[q * each : (q + 1) * each]
 
 
+def take_kernel(me_ref, weights_ref, out_ref):
+    out_ref[...] = weights_ref[0]
+
+
+def stay_kernel(in_ref, out_ref):
+    pass
+
+
 def keep_kernel(*refs):
     sem = refs[-1]
     parts, outs = refs[: len(refs) // 2], refs[len(refs) // 2 : -1]
@@ -191,6 +207,7 @@
     column = [[o * inner + n for n in line for o in range(outer)] for line in along]
     me = lax.axis_index("inner") // side
     me_ref = me.astype(jnp.int32).reshape(1)
+    hbm = pl.BlockSpec(memory_space=pltpu.HBM)
     in_hbm = functools.partial(pltpu.with_memory_space_constraint, memory_space=pltpu.HBM)
 
     def exchange(value, axes, groups):
@@ -200,12 +217,40 @@
 
     def to_column(messages):
         messages = messages.reshape(experts, 2, fold * features)
-        return exchange(messages, ("outer", "inner"), column).reshape(count, fold * features)
-
-    def from_line(weights, k):
+        got = exchange(messages, ("outer", "inner"), column)
+        got = pl.pallas_call(
+            stay_kernel,
+            in_specs=[pl.BlockSpec(memory_space=pltpu.VMEM)],
+            out_specs=pl.BlockSpec(memory_space=pltpu.VMEM),
+            out_shape=pltpu.VMEM(got.shape, got.dtype),
+            input_output_aliases={0: 0},
+            compiler_params=params(),
+            cost_estimate=cost(1, 1),
+            name="arrived",
+        )(pltpu.with_memory_space_constraint(got, pltpu.VMEM))
+        return got.reshape(count, fold * features)
+
+    def take(weights, k):
+        _, *share = weights.shape
+        return pl.pallas_call(
+            take_kernel,
+            grid_spec=pltpu.PrefetchScalarGridSpec(
+                num_scalar_prefetch=1,
+                grid=(1,),
+                in_specs=[pl.BlockSpec((1, *share), lambda n, me: (lax.rem(me[0] + k, side), 0, 0))],
+                out_specs=pl.BlockSpec(share, lambda n, me: (0, 0)),
+            ),
+            out_shape=pltpu.HBM(share, BF16),
+            compiler_params=params("arbitrary"),
+            cost_estimate=cost(1, 4 * share[0] * share[1]),
+            name="take",
+        )(me_ref, in_hbm(weights))
+
+    def from_line(weights, k, taken=None):
         pairs = [(line[n], line[(n + k) % side]) for line in along for n in range(side)]
-        share = lax.dynamic_index_in_dim(weights, (me + k) % side, 0, keepdims=False)
-        return lax.ppermute(share, "inner", pairs)
+        if taken is None:
+            taken = lax.dynamic_index_in_dim(weights, (me + k) % side, 0, keepdims=False)
+        return lax.ppermute(taken, "inner", pairs)
 
     def keep(parts, weight, name):
         return pl.pallas_call(
@@ -219,20 +264,29 @@
             name=name,
         )(*parts)
 
-    up_weights = [from_line(w_gate_up, k) for k in range(1, side)]
-    up_weights[1:2] = keep(up_weights[1:2], 20000000000, "keep_up")
-    up_weights = [in_hbm(part) for part in up_weights]
-    down_weights = keep([from_line(w_down, k) for k in range(1, side)], 20000000000, "keep_down")
+    (far,) = keep([from_line(w_gate_up, 2)], 20000000000, "keep_up")
     routes, gates = routes.T, gates.T
 
     packed = pl.pallas_call(
         functools.partial(pack_kernel, group, experts, fold),
+        in_specs=[hbm, hbm],
+        out_specs=pl.BlockSpec(memory_space=pltpu.VMEM),
+        scratch_shapes=[
+            pltpu.VMEM(routes.shape, routes.dtype),
+            pltpu.VMEM(tokens.shape, tokens.dtype),
+            pltpu.SemaphoreType.DMA((2,)),
+        ],
         out_shape=jax.ShapeDtypeStruct((count, fold * features), BF16),
         compiler_params=params(),
         cost_estimate=cost(4 * slots * rows * features, 2 * slots * features),
         name="pack",
-    )(routes, tokens)
+    )(in_hbm(routes), in_hbm(tokens))
+    packed, up_late, down_late = lax.optimization_barrier((packed, w_gate_up, w_down))
     arrived = to_column(packed)
+    near = [from_line(up_late, k, take(up_late, k)) for k in (1, 3)]
+    up_weights = [near[0], far, near[1]]
+    up_weights = [in_hbm(part) for part in up_weights]
+    down_weights = keep([from_line(down_late, k) for k in range(1, side)], 20000000000, "keep_down")
 
     tile = columns // side
     partial_value = pl.pallas_call(

time: 158 us -> 156 us (0.987)
  Pallas kernels: 10.7 us -> 15.9 us
  local copies, waits for them, and re-layouts: 9.71 us -> 5.77 us
  waiting for transfers between devices: 69 us -> 66.4 us
    pallas_call x1 -> x5, Pallas kernels: 0.62 us -> 5.8 us  [the longest x2 4.3 us: take(): pl.pallas_call(take_kernel, grid_spec=pltpu.PrefetchScalarGridSpec(num_sc...]
    all_to_all x3, waiting for transfers between devices: 69 us -> 64.6 us  [exchange(): lax.all_to_all(value, axes, split_axis=0, concat_axis=0, tiled=True, axis...]
    reshape x2, local copies, waits for them, and re-layouts: 2.32 us -> 0.49 us  [to_column(): return got.reshape(count, fold * features)]
    ppermute x6, waiting for transfers between devices: 0.02 us -> 1.72 us  [from_line(): return lax.ppermute(taken, 'inner', pairs)]
  transfers between devices with their start and end apart: 9 -> 9, of which waited for: 3 -> 4; matrix products, arithmetic and copies ran while one was open for 3% -> 2% of each run, Pallas kernels for 4% -> 8%
where the time goes in v4:
time: 156 us; the launch traced here: 155 us
  waiting for transfers between devices  66.4 us (43%)
  starting transfers between devices  57.4 us (37%)
  Pallas kernels  15.9 us (10%)
  blocking collectives  9.15 us (6%)
  local copies, waits for them, and re-layouts  5.77 us (4%)
    all_to_all x3, waiting for transfers between devices, exchange(): lax.all_to_all(value, axes, split_axis=0, concat_axis=0, tiled=True, axis...  64.6 us
    all_to_all x3, starting transfers between devices, exchange(): lax.all_to_all(value, axes, split_axis=0, concat_axis=0, tiled=True, axis...  36.8 us
    ppermute x6, starting transfers between devices, from_line(): return lax.ppermute(taken, 'inner', pairs)  20.7 us
    all_to_all x1, blocking collectives, exchange(): lax.all_to_all(value, axes, split_axis=0, concat_axis=0, tiled=True, axis...  9.15 us
    pallas_call x2, Pallas kernels, take(): pl.pallas_call(take_kernel, grid_spec=pltpu.PrefetchScalarGridSpec(num_sc...  4.3 us
    pallas_call x1, Pallas kernels, per_device(): pl.pallas_call(functools.partial(up_kernel, fold), grid_spec=pltpu.Prefet...  3.63 us
  transfers between devices with their start and end apart: 9, of which 4 were waited for; matrix products, arithmetic and copies ran while one was open for 2% of the time, Pallas kernels for 8%

profile of v4, /device:TPU:1, one launch (start us, length us, event | category | flops | bytes accessed | tf_op | source)
XLA Modules:
  0.0 154.9 jit_solution(1996290224092884720)
XLA Ops:
  0.0 2.1 %dynamic-slice_bitcast_fusion = bf16[256,1536]{1,0:T(8,128)(2,1)} fusion(bf16[4,256,1536]{2,1,0:T(8,128)(2,1)} %own_ref.2, s32[]{:T(128)S(6)} %select_n.35), kind=kLoop, calls=%fused_computation | loop fusion | bytes 1572868 | tf_op jit(solution)/shard_map/jit(dynamic_index_in_dim)/squeeze | solution.py:252
  2.1 5.6 %collective-permute-start.1 = (bf16[256,1536]{1,0:T(8,128)(2,1)}, bf16[256,1536]{1,0:T(8,128)(2,1)S(1)}, u32[]{:S(2)}, u32[]{:S(2)}) collective-permute-start(bf16[256,1536]{1,0:T(8,128)(2,1)} %dynamic-slice_bitcast_fusion), channel_id=1, source_target_pairs={{0,8},{4,12},{8,0},{12,4},{1,9},{5,13},{9,1},{13,5},{2,10},{6,14},... | collective-permute-start | bytes 2359304 | tf_op jit(solution)/shard_map/ppermute | solution.py:253
  7.7 1.5 pack.1
  9.2 1.1 reshape.29
  10.3 17.9 %all-to-all-start = ((bf16[128,2,1280]{2,1,0:T(2,128)(2,1)}), bf16[128,2,1280]{2,1,0:T(2,128)(2,1)S(1)}, u32[]{:S(2)}, u32[]{:S(2)}) async-start(bf16[128,2,1280]{2,1,0:T(2,128)(2,1)} %reshape.29), calls=%async_computation | async-start | bytes 1310720 | tf_op jit(solution)/shard_map/all_to_all | solution.py:214
  28.2 2.2 %take.2 = bf16[256,1536]{1,0:T(8,128)(2,1)} custom-call(s32[1]{0:T(128)} %bitcast.2.me_ref, bf16[4,256,1536]{2,1,0:T(8,128)(2,1)} %own_ref.2), custom_call_target="tpu_custom_call" | custom-call | flops 1 | bytes 1572864 | tf_op jit(solution)/shard_map/take/pallas_call | solution.py:235
  30.4 3.4 %collective-permute-start = (bf16[256,1536]{1,0:T(8,128)(2,1)}, bf16[256,1536]{1,0:T(8,128)(2,1)}, u32[]{:S(2)}, u32[]{:S(2)}) collective-permute-start(bf16[256,1536]{1,0:T(8,128)(2,1)} %take.2), channel_id=1, source_target_pairs={{0,4},{4,8},{8,12},{12,0},{1,5},{5,9},{9,13},{13,1},{2,6},{6,10},{... | collective-permute-start | bytes 2359304 | tf_op jit(solution)/shard_map/ppermute | solution.py:253
  33.8 2.1 %take.3 = bf16[256,1536]{1,0:T(8,128)(2,1)} custom-call(s32[1]{0:T(128)} %bitcast.2.me_ref, bf16[4,256,1536]{2,1,0:T(8,128)(2,1)} %own_ref.2), custom_call_target="tpu_custom_call" | custom-call | flops 1 | bytes 1572864 | tf_op jit(solution)/shard_map/take/pallas_call | solution.py:235
  35.9 3.6 %collective-permute-start.2 = (bf16[256,1536]{1,0:T(8,128)(2,1)}, bf16[256,1536]{1,0:T(8,128)(2,1)}, u32[]{:S(2)}, u32[]{:S(2)}) collective-permute-start(bf16[256,1536]{1,0:T(8,128)(2,1)} %take.3), channel_id=1, source_target_pairs={{0,12},{4,0},{8,4},{12,8},{1,13},{5,1},{9,5},{13,9},{2,14},{6,2},{... | collective-permute-start | bytes 2359304 | tf_op jit(solution)/shard_map/ppermute | solution.py:253
  40.5 3.3 %collective-permute-start.5 = (bf16[768,256]{1,0:T(8,128)(2,1)}, bf16[768,256]{1,0:T(8,128)(2,1)S(1)}, u32[]{:S(2)}, u32[]{:S(2)}) collective-permute-start(bf16[768,256]{1,0:T(8,128)(2,1)} %get-tuple-element.25), channel_id=1, source_target_pairs={{0,12},{4,0},{8,4},{12,8},{1,13},{5,1},{9,5},{13,9},{2,14},{6,2},{... | collective-permute-start | bytes 1179656 | tf_op jit(solution)/shard_map/ppermute | solution.py:253
  43.9 2.0 %collective-permute-start.4 = (bf16[768,256]{1,0:T(8,128)(2,1)}, bf16[768,256]{1,0:T(8,128)(2,1)S(1)}, u32[]{:S(2)}, u32[]{:S(2)}) collective-permute-start(bf16[768,256]{1,0:T(8,128)(2,1)} %get-tuple-element.26), channel_id=1, source_target_pairs={{0,8},{4,12},{8,0},{12,4},{1,9},{5,13},{9,1},{13,5},{2,10},{6,14},... | collective-permute-start | bytes 1179656 | tf_op jit(solution)/shard_map/ppermute | solution.py:253
  46.0 2.7 %collective-permute-start.3 = (bf16[768,256]{1,0:T(8,128)(2,1)S(1)}, bf16[768,256]{1,0:T(8,128)(2,1)S(1)}, u32[]{:S(2)}, u32[]{:S(2)}) collective-permute-start(bf16[768,256]{1,0:T(8,128)(2,1)S(1)} %get-tuple-element.27), channel_id=1, source_target_pairs={{0,4},{4,8},{8,12},{12,0},{1,5},{5,9},{9,13},{13,1},{2,6},{6,10},{... | collective-permute-start | bytes 1179656 | tf_op jit(solution)/shard_map/ppermute | solution.py:253
  49.6 17.0 %all-to-all-done.in_ref = bf16[128,2,1280]{2,1,0:T(2,128)(2,1)S(1)} async-done(((bf16[128,2,1280]{2,1,0:T(2,128)(2,1)}), bf16[128,2,1280]{2,1,0:T(2,128)(2,1)S(1)}, u32[]{:S(2)}, u32[]{:S(2)}) %all-to-all-start) | async-done | bytes 655392 | tf_op jit(solution)/shard_map/all_to_all | solution.py:214
  66.8 3.6 %gate_up.1 = bf16[4,320,384]{2,1,0:T(8,128)(2,1)} custom-call(s32[1]{0:T(128)} %bitcast.2.me_ref, bf16[256,1280]{1,0:T(8,128)(2,1)S(1)} %reshape.30.arrived_ref, bf16[4,256,1536]{2,1,0:T(8,128)(2,1)} %own_ref.2, bf16[256,1536]{1,0:T(8,128)(2,1)} %collective-permute-done.refs_0_, bf16[256,1536]{1,0:T(8,128)(2,1)} %keep_up.1.refs_1_, ...), custom_call_target="tpu_custom_call" | custom-call | flops 1006632960 | bytes 3145728 | tf_op jit(solution)/shard_map/gate_up/pallas_call | solution.py:292
  70.5 4.0 %all-to-all-start.1 = ((bf16[4,320,384]{2,1,0:T(8,128)(2,1)}), bf16[4,320,384]{2,1,0:T(8,128)(2,1)S(1)}, u32[]{:S(2)}, u32[]{:S(2)}) async-start(bf16[4,320,384]{2,1,0:T(8,128)(2,1)} %gate_up.1), calls=%async_computation.1 | async-start | bytes 1966080 | tf_op jit(solution)/shard_map/all_to_all | solution.py:214
  74.5 1.7 %collective-permute-done.3.refs_0_ = bf16[768,256]{1,0:T(8,128)(2,1)S(1)} collective-permute-done((bf16[768,256]{1,0:T(8,128)(2,1)S(1)}, bf16[768,256]{1,0:T(8,128)(2,1)S(1)}, u32[]{:S(2)}, u32[]{:S(2)}) %collective-permute-start.3) | collective-permute-done | bytes 393248 | tf_op jit(solution)/shard_map/ppermute | solution.py:253
  76.2 1.1 keep_down.1
  77.3 9.9 %all-to-all-done.1 = bf16[4,320,384]{2,1,0:T(8,128)(2,1)S(1)} async-done(((bf16[4,320,384]{2,1,0:T(8,128)(2,1)}), bf16[4,320,384]{2,1,0:T(8,128)(2,1)S(1)}, u32[]{:S(2)}, u32[]{:S(2)}) %all-to-all-start.1) | async-done | bytes 983072 | tf_op jit(solution)/shard_map/all_to_all | solution.py:214
  88.1 9.1 %all_to_all.25.hidden_ref = bf16[4,160,384]{2,1,0:T(8,128)(2,1)S(1)} all-to-all(bf16[4,160,384]{2,1,0:T(8,128)(2,1)S(1)} %hidden.1), channel_id=1, replica_groups={{0,1,2,3},{4,5,6,7},{8,9,10,11},{12,13,14,15},{16,17,18,19},{20,21,22,2..., dimensions={0} | all-to-all | bytes 983040 | tf_op jit(solution)/shard_map/all_to_all | solution.py:214
  97.2 2.1 %down.1 = bf16[256,1280]{1,0:T(8,128)(2,1)S(1)} custom-call(s32[1]{0:T(128)} %bitcast.2.me_ref, bf16[4,160,384]{2,1,0:T(8,128)(2,1)S(1)} %all_to_all.25.hidden_ref, bf16[4,768,256]{2,1,0:T(8,128)(2,1)} %own_ref.3, bf16[768,256]{1,0:T(8,128)(2,1)} %get-tuple-element.22.refs_0_, bf16[768,256]{1,0:T(8,128)(2,1)} %get-tuple-element.23.refs_1_, ...), custom_call_target="tpu_custom_call" | custom-call | flops 503316480 | bytes 1572864 | tf_op jit(solution)/shard_map/down/pallas_call | solution.py:325
  99.3 1.1 reshape.32
  100.4 14.9 %all-to-all-start.3 = ((bf16[128,2,1280]{2,1,0:T(2,128)(2,1)}), bf16[128,2,1280]{2,1,0:T(2,128)(2,1)S(1)}, u32[]{:S(2)}, u32[]{:S(2)}) async-start(bf16[128,2,1280]{2,1,0:T(2,128)(2,1)} %reshape.32), calls=%async_computation.3 | async-start | bytes 1310720 | tf_op jit(solution)/shard_map/all_to_all | solution.py:214
  115.8 37.7 %all-to-all-done.3.in_ref = bf16[128,2,1280]{2,1,0:T(2,128)(2,1)S(1)} async-done(((bf16[128,2,1280]{2,1,0:T(2,128)(2,1)}), bf16[128,2,1280]{2,1,0:T(2,128)(2,1)S(1)}, u32[]{:S(2)}, u32[]{:S(2)}) %all-to-all-start.3) | async-done | bytes 655392 | tf_op jit(solution)/shard_map/all_to_all | solution.py:214
  153.8 1.1 mix.1
  (21 shorter events, 3.8 us)
Async XLA Ops:
  2.1 43.9 %collective-permute-start.1 = (bf16[256,1536]{1,0:T(8,128)(2,1)}, bf16[256,1536]{1,0:T(8,128)(2,1)S(1)}, u32[]{:S(2)}, u32[]{:S(2)}) collective-permute-start(bf16[256,1536]{1,0:T(8,128)(2,1)} %dynamic-slice_bitcast_fusion), channel_id=1, source_target_pairs={{0,8},{4,12},{8,0},{12,4},{1,9},{5,13},{9,1},{13,5},{2,10},{6,14},... | collective-permute-start | bytes 2359304 | tf_op jit(solution)/shard_map/ppermute | solution.py:253
  10.3 56.2 %all-to-all-start = ((bf16[128,2,1280]{2,1,0:T(2,128)(2,1)}), bf16[128,2,1280]{2,1,0:T(2,128)(2,1)S(1)}, u32[]{:S(2)}, u32[]{:S(2)}) async-start(bf16[128,2,1280]{2,1,0:T(2,128)(2,1)} %reshape.29), calls=%async_computation | async-start | bytes 1310720 | tf_op jit(solution)/shard_map/all_to_all | solution.py:214
  28.2 11.3 %copy-start.3 = (bf16[4,768,256]{2,1,0:T(8,128)(2,1)S(1)}, bf16[4,768,256]{2,1,0:T(8,128)(2,1)}, u32[]{:S(2)}) copy-start(bf16[4,768,256]{2,1,0:T(8,128)(2,1)} %own_ref.3) | copy-start | bytes 4718596
  30.4 36.4 %collective-permute-start = (bf16[256,1536]{1,0:T(8,128)(2,1)}, bf16[256,1536]{1,0:T(8,128)(2,1)}, u32[]{:S(2)}, u32[]{:S(2)}) collective-permute-start(bf16[256,1536]{1,0:T(8,128)(2,1)} %take.2), channel_id=1, source_target_pairs={{0,4},{4,8},{8,12},{12,0},{1,5},{5,9},{9,13},{13,1},{2,6},{6,10},{... | collective-permute-start | bytes 2359304 | tf_op jit(solution)/shard_map/ppermute | solution.py:253
  35.9 30.9 %collective-permute-start.2 = (bf16[256,1536]{1,0:T(8,128)(2,1)}, bf16[256,1536]{1,0:T(8,128)(2,1)}, u32[]{:S(2)}, u32[]{:S(2)}) collective-permute-start(bf16[256,1536]{1,0:T(8,128)(2,1)} %take.3), channel_id=1, source_target_pairs={{0,12},{4,0},{8,4},{12,8},{1,13},{5,1},{9,5},{13,9},{2,14},{6,2},{... | collective-permute-start | bytes 2359304 | tf_op jit(solution)/shard_map/ppermute | solution.py:253
  40.5 33.9 %collective-permute-start.5 = (bf16[768,256]{1,0:T(8,128)(2,1)}, bf16[768,256]{1,0:T(8,128)(2,1)S(1)}, u32[]{:S(2)}, u32[]{:S(2)}) collective-permute-start(bf16[768,256]{1,0:T(8,128)(2,1)} %get-tuple-element.25), channel_id=1, source_target_pairs={{0,12},{4,0},{8,4},{12,8},{1,13},{5,1},{9,5},{13,9},{2,14},{6,2},{... | collective-permute-start | bytes 1179656 | tf_op jit(solution)/shard_map/ppermute | solution.py:253
  43.9 30.6 %collective-permute-start.4 = (bf16[768,256]{1,0:T(8,128)(2,1)}, bf16[768,256]{1,0:T(8,128)(2,1)S(1)}, u32[]{:S(2)}, u32[]{:S(2)}) collective-permute-start(bf16[768,256]{1,0:T(8,128)(2,1)} %get-tuple-element.26), channel_id=1, source_target_pairs={{0,8},{4,12},{8,0},{12,4},{1,9},{5,13},{9,1},{13,5},{2,10},{6,14},... | collective-permute-start | bytes 1179656 | tf_op jit(solution)/shard_map/ppermute | solution.py:253
  46.0 30.2 %collective-permute-start.3 = (bf16[768,256]{1,0:T(8,128)(2,1)S(1)}, bf16[768,256]{1,0:T(8,128)(2,1)S(1)}, u32[]{:S(2)}, u32[]{:S(2)}) collective-permute-start(bf16[768,256]{1,0:T(8,128)(2,1)S(1)} %get-tuple-element.27), channel_id=1, source_target_pairs={{0,4},{4,8},{8,12},{12,0},{1,5},{5,9},{9,13},{13,1},{2,6},{6,10},{... | collective-permute-start | bytes 1179656 | tf_op jit(solution)/shard_map/ppermute | solution.py:253
  70.5 16.7 %all-to-all-start.1 = ((bf16[4,320,384]{2,1,0:T(8,128)(2,1)}), bf16[4,320,384]{2,1,0:T(8,128)(2,1)S(1)}, u32[]{:S(2)}, u32[]{:S(2)}) async-start(bf16[4,320,384]{2,1,0:T(8,128)(2,1)} %gate_up.1), calls=%async_computation.1 | async-start | bytes 1966080 | tf_op jit(solution)/shard_map/all_to_all | solution.py:214
  97.2 18.1 %copy-start.1 = (s32[128,8]{0,1:T(8,128)S(1)}, s32[128,8]{0,1:T(8,128)}, u32[]{:S(2)}) copy-start(s32[128,8]{0,1:T(8,128)} %param.6) | copy-start | bytes 12292
  97.2 18.1 %copy-start.2 = (f32[128,8]{0,1:T(8,128)S(1)}, f32[128,8]{0,1:T(8,128)}, u32[]{:S(2)}) copy-start(f32[128,8]{0,1:T(8,128)} %param.7) | copy-start | bytes 12292
  99.3 54.5 %copy-start = (bf16[128,256]{1,0:T(8,128)(2,1)S(1)}, bf16[128,256]{1,0:T(8,128)(2,1)}, u32[]{:S(2)}) copy-start(bf16[128,256]{1,0:T(8,128)(2,1)} %tokens_ref.1) | copy-start | bytes 196612
  100.4 53.2 %all-to-all-start.3 = ((bf16[128,2,1280]{2,1,0:T(2,128)(2,1)}), bf16[128,2,1280]{2,1,0:T(2,128)(2,1)S(1)}, u32[]{:S(2)}, u32[]{:S(2)}) async-start(bf16[128,2,1280]{2,1,0:T(2,128)(2,1)} %reshape.32), calls=%async_computation.3 | async-start | bytes 1310720 | tf_op jit(solution)/shard_map/all_to_all | solution.py:214

commit v5 on v4

--- a/solution.py
+++ b/solution.py
@@ -155,10 +155,6 @@
     out_ref[...] = weights_ref[0]
 
 
-def stay_kernel(in_ref, out_ref):
-    pass
-
-
 def keep_kernel(*refs):
     sem = refs[-1]
     parts, outs = refs[: len(refs) // 2], refs[len(refs) // 2 : -1]
@@ -218,16 +214,6 @@
     def to_column(messages):
         messages = messages.reshape(experts, 2, fold * features)
         got = exchange(messages, ("outer", "inner"), column)
-        got = pl.pallas_call(
-            stay_kernel,
-            in_specs=[pl.BlockSpec(memory_space=pltpu.VMEM)],
-            out_specs=pl.BlockSpec(memory_space=pltpu.VMEM),
-            out_shape=pltpu.VMEM(got.shape, got.dtype),
-            input_output_aliases={0: 0},
-            compiler_params=params(),
-            cost_estimate=cost(1, 1),
-            name="arrived",
-        )(pltpu.with_memory_space_constraint(got, pltpu.VMEM))
         return got.reshape(count, fold * features)
 
     def take(weights, k):

time: 156 us -> 156 us (level)
  local copies, waits for them, and re-layouts: 5.77 us -> 7.58 us
    reshape x2, local copies, waits for them, and re-layouts: 0.49 us -> 2.32 us  [to_column(): return got.reshape(count, fold * features)]
    ppermute x6, waiting for transfers between devices: 1.72 us -> 0.08 us  [from_line(): return lax.ppermute(taken, 'inner', pairs)]
  transfers between devices with their start and end apart: 9 -> 9, of which waited for: 4 -> 4; matrix products, arithmetic and copies ran while one was open for 2% -> 3% of each run, Pallas kernels for 8% -> 8%
where the time goes in v5:
time: 156 us; the launch traced here: 155 us
  waiting for transfers between devices  66.1 us (42%)
  starting transfers between devices  56.2 us (36%)
  Pallas kernels  15.9 us (10%)
  blocking collectives  9.15 us (6%)
  local copies, waits for them, and re-layouts  7.58 us (5%)
    all_to_all x3, waiting for transfers between devices, exchange(): lax.all_to_all(value, axes, split_axis=0, concat_axis=0, tiled=True, axis...  66 us
    all_to_all x3, starting transfers between devices, exchange(): lax.all_to_all(value, axes, split_axis=0, concat_axis=0, tiled=True, axis...  35.5 us
    ppermute x6, starting transfers between devices, from_line(): return lax.ppermute(taken, 'inner', pairs)  20.7 us
    all_to_all x1, blocking collectives, exchange(): lax.all_to_all(value, axes, split_axis=0, concat_axis=0, tiled=True, axis...  9.15 us
    pallas_call x2, Pallas kernels, take(): pl.pallas_call(take_kernel, grid_spec=pltpu.PrefetchScalarGridSpec(num_sc...  4.31 us
    pallas_call x1, Pallas kernels, per_device(): pl.pallas_call(functools.partial(up_kernel, fold), grid_spec=pltpu.Prefet...  3.61 us
  transfers between devices with their start and end apart: 9, of which 4 were waited for; matrix products, arithmetic and copies ran while one was open for 3% of the time, Pallas kernels for 8%

profile of v5, /device:TPU:1, one launch (start us, length us, event | category | flops | bytes accessed | tf_op | source)
XLA Modules:
  0.0 155.1 jit_solution(7091594355795145637)
XLA Ops:
  0.0 2.1 %dynamic-slice_bitcast_fusion = bf16[256,1536]{1,0:T(8,128)(2,1)} fusion(bf16[4,256,1536]{2,1,0:T(8,128)(2,1)} %own_ref.2, s32[]{:T(128)S(6)} %select_n.35), kind=kLoop, calls=%fused_computation | loop fusion | bytes 1572868 | tf_op jit(solution)/shard_map/jit(dynamic_index_in_dim)/squeeze | solution.py:238
  2.1 5.6 %collective-permute-start.1 = (bf16[256,1536]{1,0:T(8,128)(2,1)}, bf16[256,1536]{1,0:T(8,128)(2,1)S(1)}, u32[]{:S(2)}, u32[]{:S(2)}) collective-permute-start(bf16[256,1536]{1,0:T(8,128)(2,1)} %dynamic-slice_bitcast_fusion), channel_id=1, source_target_pairs={{0,8},{4,12},{8,0},{12,4},{1,9},{5,13},{9,1},{13,5},{2,10},{6,14},... | collective-permute-start | bytes 2359304 | tf_op jit(solution)/shard_map/ppermute | solution.py:239
  7.7 1.5 pack.1
  9.2 1.1 reshape.29
  10.3 18.3 %all-to-all-start = ((bf16[128,2,1280]{2,1,0:T(2,128)(2,1)}), bf16[128,2,1280]{2,1,0:T(2,128)(2,1)}, u32[]{:S(2)}, u32[]{:S(2)}) async-start(bf16[128,2,1280]{2,1,0:T(2,128)(2,1)} %reshape.29), calls=%async_computation | async-start | bytes 1310720 | tf_op jit(solution)/shard_map/all_to_all | solution.py:210
  28.6 2.2 %take.2 = bf16[256,1536]{1,0:T(8,128)(2,1)} custom-call(s32[1]{0:T(128)} %bitcast.2.me_ref, bf16[4,256,1536]{2,1,0:T(8,128)(2,1)} %own_ref.2), custom_call_target="tpu_custom_call" | custom-call | flops 1 | bytes 1572864 | tf_op jit(solution)/shard_map/take/pallas_call | solution.py:221
  30.8 3.4 %collective-permute-start = (bf16[256,1536]{1,0:T(8,128)(2,1)}, bf16[256,1536]{1,0:T(8,128)(2,1)}, u32[]{:S(2)}, u32[]{:S(2)}) collective-permute-start(bf16[256,1536]{1,0:T(8,128)(2,1)} %take.2), channel_id=1, source_target_pairs={{0,4},{4,8},{8,12},{12,0},{1,5},{5,9},{9,13},{13,1},{2,6},{6,10},{... | collective-permute-start | bytes 2359304 | tf_op jit(solution)/shard_map/ppermute | solution.py:239
  34.2 2.1 %take.3 = bf16[256,1536]{1,0:T(8,128)(2,1)} custom-call(s32[1]{0:T(128)} %bitcast.2.me_ref, bf16[4,256,1536]{2,1,0:T(8,128)(2,1)} %own_ref.2), custom_call_target="tpu_custom_call" | custom-call | flops 1 | bytes 1572864 | tf_op jit(solution)/shard_map/take/pallas_call | solution.py:221
  36.3 3.6 %collective-permute-start.2 = (bf16[256,1536]{1,0:T(8,128)(2,1)}, bf16[256,1536]{1,0:T(8,128)(2,1)}, u32[]{:S(2)}, u32[]{:S(2)}) collective-permute-start(bf16[256,1536]{1,0:T(8,128)(2,1)} %take.3), channel_id=1, source_target_pairs={{0,12},{4,0},{8,4},{12,8},{1,13},{5,1},{9,5},{13,9},{2,14},{6,2},{... | collective-permute-start | bytes 2359304 | tf_op jit(solution)/shard_map/ppermute | solution.py:239
  40.9 3.3 %collective-permute-start.5 = (bf16[768,256]{1,0:T(8,128)(2,1)}, bf16[768,256]{1,0:T(8,128)(2,1)S(1)}, u32[]{:S(2)}, u32[]{:S(2)}) collective-permute-start(bf16[768,256]{1,0:T(8,128)(2,1)} %get-tuple-element.25), channel_id=1, source_target_pairs={{0,12},{4,0},{8,4},{12,8},{1,13},{5,1},{9,5},{13,9},{2,14},{6,2},{... | collective-permute-start | bytes 1179656 | tf_op jit(solution)/shard_map/ppermute | solution.py:239
  44.3 2.0 %collective-permute-start.4 = (bf16[768,256]{1,0:T(8,128)(2,1)}, bf16[768,256]{1,0:T(8,128)(2,1)S(1)}, u32[]{:S(2)}, u32[]{:S(2)}) collective-permute-start(bf16[768,256]{1,0:T(8,128)(2,1)} %get-tuple-element.26), channel_id=1, source_target_pairs={{0,8},{4,12},{8,0},{12,4},{1,9},{5,13},{9,1},{13,5},{2,10},{6,14},... | collective-permute-start | bytes 1179656 | tf_op jit(solution)/shard_map/ppermute | solution.py:239
  46.3 2.7 %collective-permute-start.3 = (bf16[768,256]{1,0:T(8,128)(2,1)S(1)}, bf16[768,256]{1,0:T(8,128)(2,1)S(1)}, u32[]{:S(2)}, u32[]{:S(2)}) collective-permute-start(bf16[768,256]{1,0:T(8,128)(2,1)S(1)} %get-tuple-element.27), channel_id=1, source_target_pairs={{0,4},{4,8},{8,12},{12,0},{1,5},{5,9},{9,13},{13,1},{2,6},{6,10},{... | collective-permute-start | bytes 1179656 | tf_op jit(solution)/shard_map/ppermute | solution.py:239
  50.0 16.7 %all-to-all-done = bf16[128,2,1280]{2,1,0:T(2,128)(2,1)} async-done(((bf16[128,2,1280]{2,1,0:T(2,128)(2,1)}), bf16[128,2,1280]{2,1,0:T(2,128)(2,1)}, u32[]{:S(2)}, u32[]{:S(2)}) %all-to-all-start) | async-done | bytes 655392 | tf_op jit(solution)/shard_map/all_to_all | solution.py:210
  66.6 2.1 %reshape.30.arrived_ref = bf16[256,1280]{1,0:T(8,128)(2,1)S(1)} reshape(bf16[128,2,1280]{2,1,0:T(2,128)(2,1)} %all-to-all-done) | data formatting | bytes 1310720 | tf_op jit(solution)/shard_map/reshape | solution.py:217
  68.7 3.6 %gate_up.1 = bf16[4,320,384]{2,1,0:T(8,128)(2,1)} custom-call(s32[1]{0:T(128)} %bitcast.2.me_ref, bf16[256,1280]{1,0:T(8,128)(2,1)S(1)} %reshape.30.arrived_ref, bf16[4,256,1536]{2,1,0:T(8,128)(2,1)} %own_ref.2, bf16[256,1536]{1,0:T(8,128)(2,1)} %collective-permute-done.refs_0_, bf16[256,1536]{1,0:T(8,128)(2,1)} %keep_up.1.refs_1_, ...), custom_call_target="tpu_custom_call" | custom-call | flops 1006632960 | bytes 3145728 | tf_op jit(solution)/shard_map/gate_up/pallas_call | solution.py:278
  72.4 4.0 %all-to-all-start.1 = ((bf16[4,320,384]{2,1,0:T(8,128)(2,1)}), bf16[4,320,384]{2,1,0:T(8,128)(2,1)S(1)}, u32[]{:S(2)}, u32[]{:S(2)}) async-start(bf16[4,320,384]{2,1,0:T(8,128)(2,1)} %gate_up.1), calls=%async_computation.1 | async-start | bytes 1966080 | tf_op jit(solution)/shard_map/all_to_all | solution.py:210
  76.4 1.1 keep_down.1
  77.5 11.6 %all-to-all-done.1 = bf16[4,320,384]{2,1,0:T(8,128)(2,1)S(1)} async-done(((bf16[4,320,384]{2,1,0:T(8,128)(2,1)}), bf16[4,320,384]{2,1,0:T(8,128)(2,1)S(1)}, u32[]{:S(2)}, u32[]{:S(2)}) %all-to-all-start.1) | async-done | bytes 983072 | tf_op jit(solution)/shard_map/all_to_all | solution.py:210
  90.0 9.1 %all_to_all.25.hidden_ref = bf16[4,160,384]{2,1,0:T(8,128)(2,1)S(1)} all-to-all(bf16[4,160,384]{2,1,0:T(8,128)(2,1)S(1)} %hidden.1), channel_id=1, replica_groups={{0,1,2,3},{4,5,6,7},{8,9,10,11},{12,13,14,15},{16,17,18,19},{20,21,22,2..., dimensions={0} | all-to-all | bytes 983040 | tf_op jit(solution)/shard_map/all_to_all | solution.py:210
  99.1 2.1 %down.1 = bf16[256,1280]{1,0:T(8,128)(2,1)S(1)} custom-call(s32[1]{0:T(128)} %bitcast.2.me_ref, bf16[4,160,384]{2,1,0:T(8,128)(2,1)S(1)} %all_to_all.25.hidden_ref, bf16[4,768,256]{2,1,0:T(8,128)(2,1)} %own_ref.3, bf16[768,256]{1,0:T(8,128)(2,1)} %get-tuple-element.22.refs_0_, bf16[768,256]{1,0:T(8,128)(2,1)} %get-tuple-element.23.refs_1_, ...), custom_call_target="tpu_custom_call" | custom-call | flops 503316480 | bytes 1572864 | tf_op jit(solution)/shard_map/down/pallas_call | solution.py:311
  101.2 1.1 reshape.32
  102.3 13.2 %all-to-all-start.3 = ((bf16[128,2,1280]{2,1,0:T(2,128)(2,1)}), bf16[128,2,1280]{2,1,0:T(2,128)(2,1)S(1)}, u32[]{:S(2)}, u32[]{:S(2)}) async-start(bf16[128,2,1280]{2,1,0:T(2,128)(2,1)} %reshape.32), calls=%async_computation.3 | async-start | bytes 1310720 | tf_op jit(solution)/shard_map/all_to_all | solution.py:210
  116.1 37.7 %all-to-all-done.3 = bf16[128,2,1280]{2,1,0:T(2,128)(2,1)S(1)} async-done(((bf16[128,2,1280]{2,1,0:T(2,128)(2,1)}), bf16[128,2,1280]{2,1,0:T(2,128)(2,1)S(1)}, u32[]{:S(2)}, u32[]{:S(2)}) %all-to-all-start.3) | async-done | bytes 655392 | tf_op jit(solution)/shard_map/all_to_all | solution.py:210
  154.1 1.1 mix.1
  (19 shorter events, 3.6 us)
Async XLA Ops:
  2.1 44.3 %collective-permute-start.1 = (bf16[256,1536]{1,0:T(8,128)(2,1)}, bf16[256,1536]{1,0:T(8,128)(2,1)S(1)}, u32[]{:S(2)}, u32[]{:S(2)}) collective-permute-start(bf16[256,1536]{1,0:T(8,128)(2,1)} %dynamic-slice_bitcast_fusion), channel_id=1, source_target_pairs={{0,8},{4,12},{8,0},{12,4},{1,9},{5,13},{9,1},{13,5},{2,10},{6,14},... | collective-permute-start | bytes 2359304 | tf_op jit(solution)/shard_map/ppermute | solution.py:239
  10.3 56.3 %all-to-all-start = ((bf16[128,2,1280]{2,1,0:T(2,128)(2,1)}), bf16[128,2,1280]{2,1,0:T(2,128)(2,1)}, u32[]{:S(2)}, u32[]{:S(2)}) async-start(bf16[128,2,1280]{2,1,0:T(2,128)(2,1)} %reshape.29), calls=%async_computation | async-start | bytes 1310720 | tf_op jit(solution)/shard_map/all_to_all | solution.py:210
  28.6 11.3 %copy-start.3 = (bf16[4,768,256]{2,1,0:T(8,128)(2,1)S(1)}, bf16[4,768,256]{2,1,0:T(8,128)(2,1)}, u32[]{:S(2)}) copy-start(bf16[4,768,256]{2,1,0:T(8,128)(2,1)} %own_ref.3) | copy-start | bytes 4718596
  30.8 37.9 %collective-permute-start = (bf16[256,1536]{1,0:T(8,128)(2,1)}, bf16[256,1536]{1,0:T(8,128)(2,1)}, u32[]{:S(2)}, u32[]{:S(2)}) collective-permute-start(bf16[256,1536]{1,0:T(8,128)(2,1)} %take.2), channel_id=1, source_target_pairs={{0,4},{4,8},{8,12},{12,0},{1,5},{5,9},{9,13},{13,1},{2,6},{6,10},{... | collective-permute-start | bytes 2359304 | tf_op jit(solution)/shard_map/ppermute | solution.py:239
  36.3 32.4 %collective-permute-start.2 = (bf16[256,1536]{1,0:T(8,128)(2,1)}, bf16[256,1536]{1,0:T(8,128)(2,1)}, u32[]{:S(2)}, u32[]{:S(2)}) collective-permute-start(bf16[256,1536]{1,0:T(8,128)(2,1)} %take.3), channel_id=1, source_target_pairs={{0,12},{4,0},{8,4},{12,8},{1,13},{5,1},{9,5},{13,9},{2,14},{6,2},{... | collective-permute-start | bytes 2359304 | tf_op jit(solution)/shard_map/ppermute | solution.py:239
  40.9 35.4 %collective-permute-start.5 = (bf16[768,256]{1,0:T(8,128)(2,1)}, bf16[768,256]{1,0:T(8,128)(2,1)S(1)}, u32[]{:S(2)}, u32[]{:S(2)}) collective-permute-start(bf16[768,256]{1,0:T(8,128)(2,1)} %get-tuple-element.25), channel_id=1, source_target_pairs={{0,12},{4,0},{8,4},{12,8},{1,13},{5,1},{9,5},{13,9},{2,14},{6,2},{... | collective-permute-start | bytes 1179656 | tf_op jit(solution)/shard_map/ppermute | solution.py:239
  44.3 32.1 %collective-permute-start.4 = (bf16[768,256]{1,0:T(8,128)(2,1)}, bf16[768,256]{1,0:T(8,128)(2,1)S(1)}, u32[]{:S(2)}, u32[]{:S(2)}) collective-permute-start(bf16[768,256]{1,0:T(8,128)(2,1)} %get-tuple-element.26), channel_id=1, source_target_pairs={{0,8},{4,12},{8,0},{12,4},{1,9},{5,13},{9,1},{13,5},{2,10},{6,14},... | collective-permute-start | bytes 1179656 | tf_op jit(solution)/shard_map/ppermute | solution.py:239
  46.3 30.1 %collective-permute-start.3 = (bf16[768,256]{1,0:T(8,128)(2,1)S(1)}, bf16[768,256]{1,0:T(8,128)(2,1)S(1)}, u32[]{:S(2)}, u32[]{:S(2)}) collective-permute-start(bf16[768,256]{1,0:T(8,128)(2,1)S(1)} %get-tuple-element.27), channel_id=1, source_target_pairs={{0,4},{4,8},{8,12},{12,0},{1,5},{5,9},{9,13},{13,1},{2,6},{6,10},{... | collective-permute-start | bytes 1179656 | tf_op jit(solution)/shard_map/ppermute | solution.py:239
  72.4 16.7 %all-to-all-start.1 = ((bf16[4,320,384]{2,1,0:T(8,128)(2,1)}), bf16[4,320,384]{2,1,0:T(8,128)(2,1)S(1)}, u32[]{:S(2)}, u32[]{:S(2)}) async-start(bf16[4,320,384]{2,1,0:T(8,128)(2,1)} %gate_up.1), calls=%async_computation.1 | async-start | bytes 1966080 | tf_op jit(solution)/shard_map/all_to_all | solution.py:210
  99.1 16.4 %copy-start.1 = (s32[128,8]{0,1:T(8,128)S(1)}, s32[128,8]{0,1:T(8,128)}, u32[]{:S(2)}) copy-start(s32[128,8]{0,1:T(8,128)} %param.6) | copy-start | bytes 12292
  99.1 16.4 %copy-start.2 = (f32[128,8]{0,1:T(8,128)S(1)}, f32[128,8]{0,1:T(8,128)}, u32[]{:S(2)}) copy-start(f32[128,8]{0,1:T(8,128)} %param.7) | copy-start | bytes 12292
  101.2 52.9 %copy-start = (bf16[128,256]{1,0:T(8,128)(2,1)S(1)}, bf16[128,256]{1,0:T(8,128)(2,1)}, u32[]{:S(2)}) copy-start(bf16[128,256]{1,0:T(8,128)(2,1)} %tokens_ref.1) | copy-start | bytes 196612
  102.3 51.5 %all-to-all-start.3 = ((bf16[128,2,1280]{2,1,0:T(2,128)(2,1)}), bf16[128,2,1280]{2,1,0:T(2,128)(2,1)S(1)}, u32[]{:S(2)}, u32[]{:S(2)}) async-start(bf16[128,2,1280]{2,1,0:T(2,128)(2,1)} %reshape.32), calls=%async_computation.3 | async-start | bytes 1310720 | tf_op jit(solution)/shard_map/all_to_all | solution.py:210

commit v6 on v5

--- a/solution.py
+++ b/solution.py
@@ -53,7 +53,7 @@
         load.start()
     for load in loads:
         load.wait()
-    count = packed_ref.shape[0]
+    count = 2 * packed_ref.shape[0]
     features = tokens_ref.shape[1]
     code = slot_codes(routed(routes_ref, experts)).astype(BF16)
     expert, first = message_rows(group, (count, 1), 0, fold)
@@ -62,7 +62,8 @@
     tokens = tokens_ref[...]
     for q in range(fold):
         placing = jnp.where(seen == q, 1.0, 0.0).astype(BF16)
-        packed_ref[:, q * features : (q + 1) * features] = dot(placing, tokens).astype(BF16)
+        rows = dot(placing, tokens).astype(BF16).reshape(count // 2, 2, features)
+        packed_ref[:, :, q * features : (q + 1) * features] = rows
 
 
 def gate_kernel(group, experts, fold, routes_ref, gates_ref, weights_ref):
@@ -133,7 +134,7 @@
     others, out_ref = refs[:-1], refs[-1]
     side, packed, width = hidden_ref.shape
     each = out_ref.shape[0] // side
-    features = out_ref.shape[1] // fold
+    features = out_ref.shape[2] // fold
     half = packed // batches
     left = jnp.concatenate([hidden_ref[b, :, : width // 2] for b in range(side)], axis=1)
     right = jnp.concatenate([hidden_ref[b, :, width // 2 :] for b in range(side)], axis=1)
@@ -146,9 +147,8 @@
         made = dot(hidden, w).astype(BF16)
         place = lax.rem(me_ref[0] + side - k, side) if k else me_ref[0]
         for q in range(fold):
-            out_ref[
-                pl.ds(pl.multiple_of(place * each, each), each), q * features : (q + 1) * features
-            ] = made[q * each : (q + 1) * each]
+            rows = made[2 * q * each : 2 * (q + 1) * each].reshape(each, 2, features)
+            out_ref[pl.ds(place * each, each), :, q * features : (q + 1) * features] = rows
 
 
 def take_kernel(me_ref, weights_ref, out_ref):
@@ -262,7 +262,7 @@
             pltpu.VMEM(tokens.shape, tokens.dtype),
             pltpu.SemaphoreType.DMA((2,)),
         ],
-        out_shape=jax.ShapeDtypeStruct((count, fold * features), BF16),
+        out_shape=jax.ShapeDtypeStruct((experts, 2, fold * features), BF16),
         compiler_params=params(),
         cost_estimate=cost(4 * slots * rows * features, 2 * slots * features),
         name="pack",
@@ -318,9 +318,9 @@
                 pl.BlockSpec((1, hidden, features), lambda n, me: (me[0], 0, 0)),
             ]
             + [pl.BlockSpec((hidden, features), lambda n, me: (0, 0))] * (side - 1),
-            out_specs=pl.BlockSpec((count, fold * features), lambda n, me: (0, 0)),
+            out_specs=pl.BlockSpec((experts, 2, fold * features), lambda n, me: (0, 0, 0)),
         ),
-        out_shape=jax.ShapeDtypeStruct((count, fold * features), BF16),
+        out_shape=jax.ShapeDtypeStruct((experts, 2, fold * features), BF16),
         compiler_params=params("arbitrary"),
         cost_estimate=cost(2 * slots * features * hidden, 8 * features * hidden),
         name="down",

time: 156 us -> 155 us (level)
  local copies, waits for them, and re-layouts: 7.58 us -> 3.59 us
  Pallas kernels: 15.9 us -> 17.8 us
    reshape x2 -> x0, local copies, waits for them, and re-layouts: 2.17 us -> none  [to_column(): messages = messages.reshape(experts, 2, fold * features)]
    reshape x2, local copies, waits for them, and re-layouts: 2.32 us -> 0.49 us  [to_column(): return got.reshape(count, fold * features)]
    ppermute x6, waiting for transfers between devices: 0.08 us -> 1.72 us  [from_line(): return lax.ppermute(taken, 'inner', pairs)]
  transfers between devices with their start and end apart: 9 -> 9, of which waited for: 4 -> 4; matrix products, arithmetic and copies ran while one was open for 3% -> 1% of each run, Pallas kernels for 8% -> 8%
where the time goes in v6:
time: 155 us
  waiting for transfers between devices  66.4 us (43%)
  starting transfers between devices  57.5 us (37%)
  Pallas kernels  17.8 us (11%)
  blocking collectives  9.15 us (6%)
  local copies, waits for them, and re-layouts  3.59 us (2%)
    all_to_all x3, waiting for transfers between devices, exchange(): lax.all_to_all(value, axes, split_axis=0, concat_axis=0, tiled=True, axis...  64.7 us
    all_to_all x3, starting transfers between devices, exchange(): lax.all_to_all(value, axes, split_axis=0, concat_axis=0, tiled=True, axis...  36.8 us
    ppermute x6, starting transfers between devices, from_line(): return lax.ppermute(taken, 'inner', pairs)  20.7 us
    all_to_all x1, blocking collectives, exchange(): lax.all_to_all(value, axes, split_axis=0, concat_axis=0, tiled=True, axis...  9.15 us
    pallas_call x2, Pallas kernels, take(): pl.pallas_call(take_kernel, grid_spec=pltpu.PrefetchScalarGridSpec(num_sc...  4.3 us
    pallas_call x1, Pallas kernels, per_device(): pl.pallas_call(functools.partial(up_kernel, fold), grid_spec=pltpu.Prefet...  3.63 us
  transfers between devices with their start and end apart: 9, of which 4 were waited for; matrix products, arithmetic and copies ran while one was open for 1% of the time, Pallas kernels for 8%

profile of v6, /device:TPU:1, one launch (start us, length us, event | category | flops | bytes accessed | tf_op | source)
XLA Modules:
  0.0 154.6 jit_solution(11277361026476303375)
XLA Ops:
  0.0 2.1 %dynamic-slice_bitcast_fusion = bf16[256,1536]{1,0:T(8,128)(2,1)} fusion(bf16[4,256,1536]{2,1,0:T(8,128)(2,1)} %own_ref.2, s32[]{:T(128)S(6)} %select_n.35), kind=kLoop, calls=%fused_computation | loop fusion | bytes 1572868 | tf_op jit(solution)/shard_map/jit(dynamic_index_in_dim)/squeeze | solution.py:238
  2.1 5.6 %collective-permute-start.1 = (bf16[256,1536]{1,0:T(8,128)(2,1)}, bf16[256,1536]{1,0:T(8,128)(2,1)S(1)}, u32[]{:S(2)}, u32[]{:S(2)}) collective-permute-start(bf16[256,1536]{1,0:T(8,128)(2,1)} %dynamic-slice_bitcast_fusion), channel_id=1, source_target_pairs={{0,8},{4,12},{8,0},{12,4},{1,9},{5,13},{9,1},{13,5},{2,10},{6,14},... | collective-permute-start | bytes 2359304 | tf_op jit(solution)/shard_map/ppermute | solution.py:239
  7.7 2.4 %pack.1 = bf16[128,2,1280]{2,1,0:T(2,128)(2,1)} custom-call(s32[8,128]{1,0:T(8,128)} %bitcast.13, bf16[128,256]{1,0:T(8,128)(2,1)} %tokens_ref.1), custom_call_target="tpu_custom_call" | custom-call | flops 167772160 | bytes 655360 | tf_op jit(solution)/shard_map/pack/pallas_call | solution.py:256
  10.1 17.9 %all-to-all-start = ((bf16[128,2,1280]{2,1,0:T(2,128)(2,1)}), bf16[128,2,1280]{2,1,0:T(2,128)(2,1)S(1)}, u32[]{:S(2)}, u32[]{:S(2)}) async-start(bf16[128,2,1280]{2,1,0:T(2,128)(2,1)} %pack.1), calls=%async_computation | async-start | bytes 1310720 | tf_op jit(solution)/shard_map/all_to_all | solution.py:210
  28.0 2.2 %take.2 = bf16[256,1536]{1,0:T(8,128)(2,1)} custom-call(s32[1]{0:T(128)} %bitcast.2.me_ref, bf16[4,256,1536]{2,1,0:T(8,128)(2,1)} %own_ref.2), custom_call_target="tpu_custom_call" | custom-call | flops 1 | bytes 1572864 | tf_op jit(solution)/shard_map/take/pallas_call | solution.py:221
  30.2 3.4 %collective-permute-start = (bf16[256,1536]{1,0:T(8,128)(2,1)}, bf16[256,1536]{1,0:T(8,128)(2,1)}, u32[]{:S(2)}, u32[]{:S(2)}) collective-permute-start(bf16[256,1536]{1,0:T(8,128)(2,1)} %take.2), channel_id=1, source_target_pairs={{0,4},{4,8},{8,12},{12,0},{1,5},{5,9},{9,13},{13,1},{2,6},{6,10},{... | collective-permute-start | bytes 2359304 | tf_op jit(solution)/shard_map/ppermute | solution.py:239
  33.6 2.1 %take.3 = bf16[256,1536]{1,0:T(8,128)(2,1)} custom-call(s32[1]{0:T(128)} %bitcast.2.me_ref, bf16[4,256,1536]{2,1,0:T(8,128)(2,1)} %own_ref.2), custom_call_target="tpu_custom_call" | custom-call | flops 1 | bytes 1572864 | tf_op jit(solution)/shard_map/take/pallas_call | solution.py:221
  35.7 3.6 %collective-permute-start.2 = (bf16[256,1536]{1,0:T(8,128)(2,1)}, bf16[256,1536]{1,0:T(8,128)(2,1)}, u32[]{:S(2)}, u32[]{:S(2)}) collective-permute-start(bf16[256,1536]{1,0:T(8,128)(2,1)} %take.3), channel_id=1, source_target_pairs={{0,12},{4,0},{8,4},{12,8},{1,13},{5,1},{9,5},{13,9},{2,14},{6,2},{... | collective-permute-start | bytes 2359304 | tf_op jit(solution)/shard_map/ppermute | solution.py:239
  39.3 1.0 dynamic-slice_bitcast_fusion.1
  40.3 3.3 %collective-permute-start.5 = (bf16[768,256]{1,0:T(8,128)(2,1)}, bf16[768,256]{1,0:T(8,128)(2,1)S(1)}, u32[]{:S(2)}, u32[]{:S(2)}) collective-permute-start(bf16[768,256]{1,0:T(8,128)(2,1)} %get-tuple-element.25), channel_id=1, source_target_pairs={{0,12},{4,0},{8,4},{12,8},{1,13},{5,1},{9,5},{13,9},{2,14},{6,2},{... | collective-permute-start | bytes 1179656 | tf_op jit(solution)/shard_map/ppermute | solution.py:239
  43.7 2.0 %collective-permute-start.4 = (bf16[768,256]{1,0:T(8,128)(2,1)}, bf16[768,256]{1,0:T(8,128)(2,1)S(1)}, u32[]{:S(2)}, u32[]{:S(2)}) collective-permute-start(bf16[768,256]{1,0:T(8,128)(2,1)} %get-tuple-element.26), channel_id=1, source_target_pairs={{0,8},{4,12},{8,0},{12,4},{1,9},{5,13},{9,1},{13,5},{2,10},{6,14},... | collective-permute-start | bytes 1179656 | tf_op jit(solution)/shard_map/ppermute | solution.py:239
  45.7 2.7 %collective-permute-start.3 = (bf16[768,256]{1,0:T(8,128)(2,1)S(1)}, bf16[768,256]{1,0:T(8,128)(2,1)S(1)}, u32[]{:S(2)}, u32[]{:S(2)}) collective-permute-start(bf16[768,256]{1,0:T(8,128)(2,1)S(1)} %get-tuple-element.27), channel_id=1, source_target_pairs={{0,4},{4,8},{8,12},{12,0},{1,5},{5,9},{9,13},{13,1},{2,6},{6,10},{... | collective-permute-start | bytes 1179656 | tf_op jit(solution)/shard_map/ppermute | solution.py:239
  48.5 0.9 keep_up.1.refs_1_
  49.4 17.0 %all-to-all-done = bf16[128,2,1280]{2,1,0:T(2,128)(2,1)S(1)} async-done(((bf16[128,2,1280]{2,1,0:T(2,128)(2,1)}), bf16[128,2,1280]{2,1,0:T(2,128)(2,1)S(1)}, u32[]{:S(2)}, u32[]{:S(2)}) %all-to-all-start) | async-done | bytes 655392 | tf_op jit(solution)/shard_map/all_to_all | solution.py:210
  66.6 3.6 %gate_up.1 = bf16[4,320,384]{2,1,0:T(8,128)(2,1)} custom-call(s32[1]{0:T(128)} %bitcast.2.me_ref, bf16[256,1280]{1,0:T(8,128)(2,1)S(1)} %reshape.23.arrived_ref, bf16[4,256,1536]{2,1,0:T(8,128)(2,1)} %own_ref.2, bf16[256,1536]{1,0:T(8,128)(2,1)} %collective-permute-done.refs_0_, bf16[256,1536]{1,0:T(8,128)(2,1)} %keep_up.1.refs_1_, ...), custom_call_target="tpu_custom_call" | custom-call | flops 1006632960 | bytes 3145728 | tf_op jit(solution)/shard_map/gate_up/pallas_call | solution.py:278
  70.2 4.0 %all-to-all-start.1 = ((bf16[4,320,384]{2,1,0:T(8,128)(2,1)}), bf16[4,320,384]{2,1,0:T(8,128)(2,1)S(1)}, u32[]{:S(2)}, u32[]{:S(2)}) async-start(bf16[4,320,384]{2,1,0:T(8,128)(2,1)} %gate_up.1), calls=%async_computation.1 | async-start | bytes 1966080 | tf_op jit(solution)/shard_map/all_to_all | solution.py:210
  74.3 1.7 %collective-permute-done.3.refs_0_ = bf16[768,256]{1,0:T(8,128)(2,1)S(1)} collective-permute-done((bf16[768,256]{1,0:T(8,128)(2,1)S(1)}, bf16[768,256]{1,0:T(8,128)(2,1)S(1)}, u32[]{:S(2)}, u32[]{:S(2)}) %collective-permute-start.3) | collective-permute-done | bytes 393248 | tf_op jit(solution)/shard_map/ppermute | solution.py:239
  76.0 1.1 keep_down.1
  77.0 9.9 %all-to-all-done.1 = bf16[4,320,384]{2,1,0:T(8,128)(2,1)S(1)} async-done(((bf16[4,320,384]{2,1,0:T(8,128)(2,1)}), bf16[4,320,384]{2,1,0:T(8,128)(2,1)S(1)}, u32[]{:S(2)}, u32[]{:S(2)}) %all-to-all-start.1) | async-done | bytes 983072 | tf_op jit(solution)/shard_map/all_to_all | solution.py:210
  87.9 9.1 %all_to_all.25.hidden_ref = bf16[4,160,384]{2,1,0:T(8,128)(2,1)S(1)} all-to-all(bf16[4,160,384]{2,1,0:T(8,128)(2,1)S(1)} %hidden.1), channel_id=1, replica_groups={{0,1,2,3},{4,5,6,7},{8,9,10,11},{12,13,14,15},{16,17,18,19},{20,21,22,2..., dimensions={0} | all-to-all | bytes 983040 | tf_op jit(solution)/shard_map/all_to_all | solution.py:210
  97.0 3.1 %down.1 = bf16[128,2,1280]{2,1,0:T(2,128)(2,1)} custom-call(s32[1]{0:T(128)} %bitcast.2.me_ref, bf16[4,160,384]{2,1,0:T(8,128)(2,1)S(1)} %all_to_all.25.hidden_ref, bf16[4,768,256]{2,1,0:T(8,128)(2,1)} %own_ref.3, bf16[768,256]{1,0:T(8,128)(2,1)} %get-tuple-element.22.refs_0_, bf16[768,256]{1,0:T(8,128)(2,1)} %get-tuple-element.23.refs_1_, ...), custom_call_target="tpu_custom_call" | custom-call | flops 503316480 | bytes 1572864 | tf_op jit(solution)/shard_map/down/pallas_call | solution.py:311
  100.1 14.9 %all-to-all-start.3 = ((bf16[128,2,1280]{2,1,0:T(2,128)(2,1)}), bf16[128,2,1280]{2,1,0:T(2,128)(2,1)S(1)}, u32[]{:S(2)}, u32[]{:S(2)}) async-start(bf16[128,2,1280]{2,1,0:T(2,128)(2,1)} %down.1), calls=%async_computation.3 | async-start | bytes 1310720 | tf_op jit(solution)/shard_map/all_to_all | solution.py:210
  115.5 37.7 %all-to-all-done.3 = bf16[128,2,1280]{2,1,0:T(2,128)(2,1)S(1)} async-done(((bf16[128,2,1280]{2,1,0:T(2,128)(2,1)}), bf16[128,2,1280]{2,1,0:T(2,128)(2,1)S(1)}, u32[]{:S(2)}, u32[]{:S(2)}) %all-to-all-start.3) | async-done | bytes 655392 | tf_op jit(solution)/shard_map/all_to_all | solution.py:210
  153.5 1.1 mix.1
  (17 shorter events, 1.9 us)
Async XLA Ops:
  2.1 43.7 %collective-permute-start.1 = (bf16[256,1536]{1,0:T(8,128)(2,1)}, bf16[256,1536]{1,0:T(8,128)(2,1)S(1)}, u32[]{:S(2)}, u32[]{:S(2)}) collective-permute-start(bf16[256,1536]{1,0:T(8,128)(2,1)} %dynamic-slice_bitcast_fusion), channel_id=1, source_target_pairs={{0,8},{4,12},{8,0},{12,4},{1,9},{5,13},{9,1},{13,5},{2,10},{6,14},... | collective-permute-start | bytes 2359304 | tf_op jit(solution)/shard_map/ppermute | solution.py:239
  10.1 56.2 %all-to-all-start = ((bf16[128,2,1280]{2,1,0:T(2,128)(2,1)}), bf16[128,2,1280]{2,1,0:T(2,128)(2,1)S(1)}, u32[]{:S(2)}, u32[]{:S(2)}) async-start(bf16[128,2,1280]{2,1,0:T(2,128)(2,1)} %pack.1), calls=%async_computation | async-start | bytes 1310720 | tf_op jit(solution)/shard_map/all_to_all | solution.py:210
  28.0 11.3 %copy-start.3 = (bf16[4,768,256]{2,1,0:T(8,128)(2,1)S(1)}, bf16[4,768,256]{2,1,0:T(8,128)(2,1)}, u32[]{:S(2)}) copy-start(bf16[4,768,256]{2,1,0:T(8,128)(2,1)} %own_ref.3) | copy-start | bytes 4718596
  30.2 36.4 %collective-permute-start = (bf16[256,1536]{1,0:T(8,128)(2,1)}, bf16[256,1536]{1,0:T(8,128)(2,1)}, u32[]{:S(2)}, u32[]{:S(2)}) collective-permute-start(bf16[256,1536]{1,0:T(8,128)(2,1)} %take.2), channel_id=1, source_target_pairs={{0,4},{4,8},{8,12},{12,0},{1,5},{5,9},{9,13},{13,1},{2,6},{6,10},{... | collective-permute-start | bytes 2359304 | tf_op jit(solution)/shard_map/ppermute | solution.py:239
  35.7 30.9 %collective-permute-start.2 = (bf16[256,1536]{1,0:T(8,128)(2,1)}, bf16[256,1536]{1,0:T(8,128)(2,1)}, u32[]{:S(2)}, u32[]{:S(2)}) collective-permute-start(bf16[256,1536]{1,0:T(8,128)(2,1)} %take.3), channel_id=1, source_target_pairs={{0,12},{4,0},{8,4},{12,8},{1,13},{5,1},{9,5},{13,9},{2,14},{6,2},{... | collective-permute-start | bytes 2359304 | tf_op jit(solution)/shard_map/ppermute | solution.py:239
  40.3 33.9 %collective-permute-start.5 = (bf16[768,256]{1,0:T(8,128)(2,1)}, bf16[768,256]{1,0:T(8,128)(2,1)S(1)}, u32[]{:S(2)}, u32[]{:S(2)}) collective-permute-start(bf16[768,256]{1,0:T(8,128)(2,1)} %get-tuple-element.25), channel_id=1, source_target_pairs={{0,12},{4,0},{8,4},{12,8},{1,13},{5,1},{9,5},{13,9},{2,14},{6,2},{... | collective-permute-start | bytes 1179656 | tf_op jit(solution)/shard_map/ppermute | solution.py:239
  43.7 30.6 %collective-permute-start.4 = (bf16[768,256]{1,0:T(8,128)(2,1)}, bf16[768,256]{1,0:T(8,128)(2,1)S(1)}, u32[]{:S(2)}, u32[]{:S(2)}) collective-permute-start(bf16[768,256]{1,0:T(8,128)(2,1)} %get-tuple-element.26), channel_id=1, source_target_pairs={{0,8},{4,12},{8,0},{12,4},{1,9},{5,13},{9,1},{13,5},{2,10},{6,14},... | collective-permute-start | bytes 1179656 | tf_op jit(solution)/shard_map/ppermute | solution.py:239
  45.7 30.2 %collective-permute-start.3 = (bf16[768,256]{1,0:T(8,128)(2,1)S(1)}, bf16[768,256]{1,0:T(8,128)(2,1)S(1)}, u32[]{:S(2)}, u32[]{:S(2)}) collective-permute-start(bf16[768,256]{1,0:T(8,128)(2,1)S(1)} %get-tuple-element.27), channel_id=1, source_target_pairs={{0,4},{4,8},{8,12},{12,0},{1,5},{5,9},{9,13},{13,1},{2,6},{6,10},{... | collective-permute-start | bytes 1179656 | tf_op jit(solution)/shard_map/ppermute | solution.py:239
  70.2 16.8 %all-to-all-start.1 = ((bf16[4,320,384]{2,1,0:T(8,128)(2,1)}), bf16[4,320,384]{2,1,0:T(8,128)(2,1)S(1)}, u32[]{:S(2)}, u32[]{:S(2)}) async-start(bf16[4,320,384]{2,1,0:T(8,128)(2,1)} %gate_up.1), calls=%async_computation.1 | async-start | bytes 1966080 | tf_op jit(solution)/shard_map/all_to_all | solution.py:210
  87.8 27.1 %copy-start.1 = (s32[128,8]{0,1:T(8,128)S(1)}, s32[128,8]{0,1:T(8,128)}, u32[]{:S(2)}) copy-start(s32[128,8]{0,1:T(8,128)} %param.6) | copy-start | bytes 12292
  87.9 27.1 %copy-start.2 = (f32[128,8]{0,1:T(8,128)S(1)}, f32[128,8]{0,1:T(8,128)}, u32[]{:S(2)}) copy-start(f32[128,8]{0,1:T(8,128)} %param.7) | copy-start | bytes 12292
  97.0 56.5 %copy-start = (bf16[128,256]{1,0:T(8,128)(2,1)S(1)}, bf16[128,256]{1,0:T(8,128)(2,1)}, u32[]{:S(2)}) copy-start(bf16[128,256]{1,0:T(8,128)(2,1)} %tokens_ref.1) | copy-start | bytes 196612
  100.1 53.2 %all-to-all-start.3 = ((bf16[128,2,1280]{2,1,0:T(2,128)(2,1)}), bf16[128,2,1280]{2,1,0:T(2,128)(2,1)S(1)}, u32[]{:S(2)}, u32[]{:S(2)}) async-start(bf16[128,2,1280]{2,1,0:T(2,128)(2,1)} %down.1), calls=%async_computation.3 | async-start | bytes 1310720 | tf_op jit(solution)/shard_map/all_to_all | solution.py:210
